TPU v7x, 32 devices: a whole 2x2x4 slice. The times are simulated.
32 devices in a mesh: dp: 4 (over x, core), tp: 8 (over z, y).
Axes of the slice: x: 2, y: 2, z: 4, core: 2. Of those that a mesh axis runs over, the one named last changes fastest.
Arguments:
- qkv_master: float32 [5120, 7168], P(('dp', 'tp')), may hold values from -0.078125 to 0.078125
- qkv_first: float32 [5120, 7168], P(('dp', 'tp')), may hold values from -0.75 to 0.75
- qkv_second: float32 [5120, 7168], P(('dp', 'tp')), may hold values from 0.001 to 0.1
- qkv_grad: bfloat16 [5120, 7168], P(('dp', 'tp')), may hold values from -6 to 6
- out_master: float32 [5120, 5120], P(('dp', 'tp')), may hold values from -0.078125 to 0.078125
- out_first: float32 [5120, 5120], P(('dp', 'tp')), may hold values from -0.75 to 0.75
- out_second: float32 [5120, 5120], P(('dp', 'tp')), may hold values from 0.001 to 0.1
- out_grad: bfloat16 [5120, 5120], P(('dp', 'tp')), may hold values from -6 to 6
- norm_gain: float32 [5120], replicated, may hold values from 0.1 to 1.9
- embed_table: bfloat16 [76032, 5120], P(('dp', 'tp')), may hold values from -6 to 6
- cache_keys: bfloat16 [32, 2048, 1024], P('dp', 'tp'), may hold values from -720 to 720
- cache_values: bfloat16 [32, 2048, 1024], P('dp', 'tp'), may hold values from -6 to 6
- cache_lengths: int32 [32], P('dp'), may hold values from 1 to 2048, as said below
- token_ids: int32 [32, 2], replicated, may hold values from 0 to 76031
Outputs:
- qkv_master_new: float32 [5120, 7168], P(('dp', 'tp'))
- qkv_first_new: float32 [5120, 7168], P(('dp', 'tp'))
- qkv_second_new: float32 [5120, 7168], P(('dp', 'tp'))
- out_master_new: float32 [5120, 5120], P(('dp', 'tp'))
- out_first_new: float32 [5120, 5120], P(('dp', 'tp'))
- out_second_new: float32 [5120, 5120], P(('dp', 'tp'))
- layer_out: bfloat16 [32, 2, 5120], P('dp', None, 'tp')
Inputs may be any that keep to these rules, and one draw needn't show every extreme that they name: `cache_lengths`: row 0 has all 2048 positions live and row 1 only one.
All inputs are finite; a program needn't handle non-finite values.
Results may differ from a plain program's by a relative error of at most 0.0035.
The roundings to bfloat16 on the way count: a program that leaves them out, or rounds other values in their place, can miss the bound.
Values may be sent and summed in bfloat16 or wider, within the bound.
No kernel may reach another device: no remote copies, remote signals or barrier semaphores. Data moves between devices by JAX's collectives and lax.ppermute only.
A program may use at most 256 MiB of HBM per device.

v0:
```python
import jax
import jax.numpy as jnp
from jax import lax
from jax.sharding import PartitionSpec as P

HEADS = 40
KV_HEADS = 8
HEAD = 128


BETA_ONE = 0.9
BETA_TWO = 0.95
LEARN_RATE = 0.004
WEIGHT_DECAY = 0.1
EPS_ADAM = 1e-08
EPS_NORM = 1e-06
CORR_ONE = 1.0 - 0.9**10
CORR_TWO = 1.0 - 0.95**10
MASK_LOW = -1e30


def adamw(master, first, second, grad):
    gradient = grad.astype(jnp.float32)
    first_new = BETA_ONE * first + (1.0 - BETA_ONE) * gradient
    second_new = BETA_TWO * second + (1.0 - BETA_TWO) * gradient * gradient
    update = first_new / CORR_ONE / (jnp.sqrt(second_new / CORR_TWO) + EPS_ADAM)
    master_new = master - LEARN_RATE * (update + WEIGHT_DECAY * master)
    return (master_new, first_new, second_new)


def on_device(
    qkv_master,
    qkv_first,
    qkv_second,
    qkv_grad,
    out_master,
    out_first,
    out_second,
    out_grad,
    norm_gain,
    embed_table,
    cache_keys,
    cache_values,
    cache_lengths,
    token_ids,
):
    qkv_master_new, qkv_first_new, qkv_second_new = adamw(
        qkv_master, qkv_first, qkv_second, qkv_grad
    )
    out_master_new, out_first_new, out_second_new = adamw(
        out_master, out_first, out_second, out_grad
    )
    qkv_half = qkv_master_new.astype(jnp.bfloat16)
    out_half = out_master_new.astype(jnp.bfloat16)
    qkv_group, out_group = (
        lax.all_to_all(qkv_half, "tp", split_axis=1, concat_axis=0, tiled=True),
        lax.all_to_all(out_half, "tp", split_axis=1, concat_axis=0, tiled=True),
    )
    qkv_cols, out_cols = (
        lax.all_gather(qkv_group, "dp", axis=0, tiled=True),
        lax.all_gather(out_group, "dp", axis=0, tiled=True),
    )
    width = embed_table.shape[1]
    vocab_rows = embed_table.shape[0]
    group_rows = cache_keys.shape[0]
    first_entry = lax.axis_index(("dp", "tp")) * vocab_rows
    local_ids = token_ids.reshape(-1) - first_entry
    selector = (local_ids[:, None] == jnp.arange(vocab_rows, dtype=jnp.int32)[None, :]).astype(
        jnp.bfloat16
    )
    partial_rows = jnp.dot(selector, embed_table, preferred_element_type=jnp.float32).reshape(
        -1, 2, width
    )
    every_row = lax.psum(partial_rows, ("dp", "tp"))
    own_inputs = lax.dynamic_slice_in_dim(
        every_row, lax.axis_index("dp") * group_rows, group_rows, 0
    )
    meansq = jnp.mean(own_inputs * own_inputs, axis=-1, keepdims=True)
    normed = (own_inputs * lax.rsqrt(meansq + EPS_NORM) * norm_gain).astype(jnp.bfloat16)
    proj_part = jnp.dot(
        normed.reshape(-1, width), qkv_cols, preferred_element_type=jnp.float32
    ).astype(jnp.bfloat16)
    projected = lax.all_gather(proj_part, "tp", axis=1, tiled=True).reshape(group_rows, 2, -1)
    group_size = HEADS // KV_HEADS
    kv_width = KV_HEADS * HEAD
    scale_factor = HEAD ** (-0.5)
    queries = projected[..., :width].reshape(group_rows, 2, KV_HEADS, group_size, HEAD)
    fresh_keys = projected[..., width : width + kv_width].reshape(group_rows, 2, KV_HEADS, HEAD)
    fresh_values = projected[..., width + kv_width :].reshape(group_rows, 2, KV_HEADS, HEAD)
    span = cache_keys.shape[1]
    old_keys = cache_keys.reshape(group_rows, span, KV_HEADS, HEAD)
    old_values = cache_values.reshape(group_rows, span, KV_HEADS, HEAD)
    cache_scores = (
        jnp.einsum("rsghd,rpgd->rsghp", queries, old_keys, preferred_element_type=jnp.float32)
        * scale_factor
    )
    position = lax.axis_index("tp") * span + jnp.arange(span, dtype=jnp.int32)
    live = (position[None, :] < cache_lengths[:, None])[:, None, None, None, :]
    cache_scores = jnp.where(live, cache_scores, MASK_LOW)
    local_top = cache_scores.max(-1)
    cache_probs = jnp.where(live, jnp.exp(cache_scores - local_top[..., None]), 0.0)
    local_total = cache_probs.sum(-1)
    local_weighted = jnp.einsum(
        "rsghp,rpgd->rsghd", cache_probs, old_values, preferred_element_type=jnp.float32
    )
    cache_top = lax.pmax(local_top, "tp")
    rescale = jnp.exp(local_top - cache_top)
    cache_total, cache_weighted = lax.psum(
        (local_total * rescale, local_weighted * rescale[..., None]), "tp"
    )
    fresh_scores = (
        jnp.einsum("rsghd,rjgd->rsghj", queries, fresh_keys, preferred_element_type=jnp.float32)
        * scale_factor
    )
    causal = jnp.arange(2, dtype=jnp.int32)[None, :] <= jnp.arange(2, dtype=jnp.int32)[:, None]
    causal = causal[None, :, None, None, :]
    fresh_scores = jnp.where(causal, fresh_scores, MASK_LOW)
    highest = jnp.maximum(cache_top, fresh_scores.max(-1))
    cache_scale = jnp.exp(cache_top - highest)
    fresh_probs = jnp.where(causal, jnp.exp(fresh_scores - highest[..., None]), 0.0)
    totals = cache_total * cache_scale + fresh_probs.sum(-1)
    weighted = cache_weighted * cache_scale[..., None]
    weighted = weighted + jnp.einsum(
        "rsghj,rjgd->rsghd", fresh_probs, fresh_values.astype(jnp.float32)
    )
    attended = (weighted / totals[..., None]).reshape(group_rows * 2, width).astype(jnp.bfloat16)
    out_width = out_cols.shape[1]
    mixed = jnp.dot(attended, out_cols, preferred_element_type=jnp.float32).reshape(
        group_rows, 2, out_width
    )
    residual_cols = lax.dynamic_slice_in_dim(
        own_inputs, lax.axis_index("tp") * out_width, out_width, 2
    )
    layer_out = (residual_cols + mixed).astype(jnp.bfloat16)
    return (
        qkv_master_new,
        qkv_first_new,
        qkv_second_new,
        out_master_new,
        out_first_new,
        out_second_new,
        layer_out,
    )


def solution(mesh):
    placed = (
        P(("dp", "tp"), None),
        P(("dp", "tp"), None),
        P(("dp", "tp"), None),
        P(("dp", "tp"), None),
        P(("dp", "tp"), None),
        P(("dp", "tp"), None),
        P(("dp", "tp"), None),
        P(("dp", "tp"), None),
        P(),
        P(("dp", "tp"), None),
        P("dp", "tp", None),
        P("dp", "tp", None),
        P("dp"),
        P(),
    )
    return jax.shard_map(
        on_device,
        mesh=mesh,
        in_specs=placed,
        out_specs=(
            P(("dp", "tp"), None),
            P(("dp", "tp"), None),
            P(("dp", "tp"), None),
            P(("dp", "tp"), None),
            P(("dp", "tp"), None),
            P(("dp", "tp"), None),
            P("dp", None, "tp"),
        ),
        check_vma=False,
    )
```

profile of v0, /device:TPU:0, one launch (start us, length us, event | category | flops | bytes accessed | tf_op | source)
XLA Modules:
  0.0 392.8 jit_solution(7573631734353781695)
XLA Ops:
  8.0 10.9 %fusion.51 = (bf16[160,7168]{1,0:T(8,128)(2,1)S(1)}, f32[160,7168]{1,0:T(8,128)}, f32[160,7168]{1,0:T(8,128)}, f32[160,7168]{1,0:T(8,128)}) fusion(f32[160,7168]{1,0:T(8,128)} %param.14, bf16[160,7168]{1,0:T(8,128)(2,1)} %param.17, f32[160,7168]{1,0:T(8,128)} %param.15, f32[160,7168]{1,0:T(8,128)} %param.16), kind=kLoop, calls=%fused_computation.63 | loop fusion | flops 19496960 | bytes 32112640 | tf_op jit(solution)/shard_map/convert_element_type | solution.py:53
  18.9 0.0 copy-start.5
  18.9 1.6 copy.103
  20.5 7.3 %all-to-all-start = ((bf16[160,8,896]{2,0,1:T(8,128)(2,1)}), bf16[160,8,896]{2,0,1:T(8,128)(2,1)S(1)}, u32[]{:S(2)}, u32[]{:S(2)}) async-start(bf16[160,8,896]{2,0,1:T(8,128)(2,1)} %bitcast.93), calls=%async_computation | async-start | bytes 4587520 | tf_op jit(solution)/shard_map/all_to_all | solution.py:56
  27.8 0.0 all-reduce.3.cloned.1.call-start
  27.8 0.0 copy-done.5
  27.9 0.1 copy.50
  27.9 0.1 sub.45
  28.0 11.1 %fusion.37 = f32[64,5120]{1,0:T(8,128)} fusion(bf16[2376,5120]{1,0:T(8,128)(2,1)} %param.23, s32[64]{0:T(128)S(1)} %sub.45), kind=kOutput, calls=%fused_computation.38 | convolution fusion | flops 1557287424 | bytes 25641216 | tf_op jit(solution)/shard_map/dot_general | solution.py:71
  39.1 3.0 reshape.110
  42.1 2.8 copy.51
  44.9 0.0 all-reduce.3.cloned.1.call-update
  44.9 0.0 all-gather.3.cloned.1.call-start
  45.0 40.5 %all-to-all-done = bf16[160,8,896]{2,0,1:T(8,128)(2,1)S(1)} async-done(((bf16[160,8,896]{2,0,1:T(8,128)(2,1)}), bf16[160,8,896]{2,0,1:T(8,128)(2,1)S(1)}, u32[]{:S(2)}, u32[]{:S(2)}) %all-to-all-start) | async-done | bytes 2293792 | tf_op jit(solution)/shard_map/all_to_all | solution.py:56
  85.5 0.0 copy-start.1
  85.5 1.4 copy-done.1
  87.0 0.0 all-gather.3.cloned.1.call-update
  87.0 8.1 %fusion.47 = (bf16[160,5120]{1,0:T(8,128)(2,1)S(1)}, f32[160,5120]{1,0:T(8,128)}, f32[160,5120]{1,0:T(8,128)}, f32[160,5120]{1,0:T(8,128)}) fusion(f32[160,5120]{1,0:T(8,128)} %param.18, bf16[160,5120]{1,0:T(8,128)(2,1)} %param.21, f32[160,5120]{1,0:T(8,128)} %param.19, f32[160,5120]{1,0:T(8,128)} %param.20), kind=kLoop, calls=%fused_computation.61 | loop fusion | flops 13926400 | bytes 22937600 | tf_op jit(solution)/shard_map/convert_element_type | solution.py:54
  95.0 1.4 copy.104
  96.4 4.4 %all-to-all-start.1 = ((bf16[160,8,640]{2,0,1:T(8,128)(2,1)}), bf16[160,8,640]{2,0,1:T(8,128)(2,1)S(1)}, u32[]{:S(2)}, u32[]{:S(2)}) async-start(bf16[160,8,640]{2,0,1:T(8,128)(2,1)} %bitcast.74), calls=%async_computation.1 | async-start | bytes 3276800 | tf_op jit(solution)/shard_map/all_to_all | solution.py:57
  100.9 0.0 all-reduce.5.cloned.1.call-start
  100.9 0.0 copy-start.3
  100.9 5.4 %copy.75 = bf16[256,8,8,128]{3,2,1,0:T(8,128)(2,1)} copy(bf16[256,8,8,128]{3,1,2,0:T(8,128)(2,1)} %bitcast.97) | data formatting | bytes 8388608
  106.4 0.0 copy-done.3
  106.4 0.0 copy-start.6
  106.4 3.0 copy.76
  109.4 0.0 copy-done.6
  109.4 0.1 broadcast_compare_fusion
  109.5 0.0 copy-start
  109.5 4.7 %bitcast_bitcast_fusion.1 = bf16[8,256,8,128,1]{3,2,1,0,4:T(8,128)(2,1)} fusion(bf16[8,256,8,128]{3,2,1,0:T(8,128)(2,1)} %bitcast.91), kind=kLoop, calls=%fused_computation.9 | loop fusion | bytes 8388608 | tf_op jit(solution)/shard_map/reshape | solution.py:91
  114.2 0.0 copy-done
  114.2 2.2 bitcast_bitcast_fusion
  116.4 109.3 %all-reduce.3.cloned.1.call-done = f32[32,2,5120]{2,0,1:T(8,128)} async-done(((f32[32,2,5120]{2,0,1:T(8,128)}), f32[32,2,5120]{2,0,1:T(8,128)}) %all-reduce.3.cloned.1.call-update) | async-done | bytes 1310736 | tf_op jit(solution)/shard_map/psum | solution.py:74
  225.7 1.1 multiply_reduce_fusion
  226.8 0.0 copy-done.4
  226.8 1.1 multiply_convert_fusion
  227.9 0.2 copy.52
  228.0 0.1 reshape.111
  228.1 0.0 all-gather.3.cloned.1.call-done
  228.2 4.9 %convolution_convert_fusion = bf16[16,896]{1,0:T(8,128)(2,1)S(1)} fusion(bf16[16,5120]{1,0:T(8,128)(2,1)S(1)} %reshape.111, bf16[5120,896]{1,0:T(8,128)(2,1)} %all-gather.3.cloned.1.call-done), kind=kOutput, calls=%fused_computation.32 | convolution fusion | flops 146814976 | bytes 9367552 | tf_op jit(solution)/shard_map/dot_general | solution.py:80
  233.0 30.9 %all_gather.10 = bf16[16,7168]{1,0:T(8,128)(2,1)S(1)} all-gather(bf16[16,896]{1,0:T(8,128)(2,1)S(1)} %convolution_convert_fusion), channel_id=1, replica_groups=mesh['dp'=4,'tp'=8] {'tp'}, dimensions={1}, use_global_device_ids=true | all-gather | bytes 258048 | tf_op jit(solution)/shard_map/all_gather | solution.py:83
  264.0 0.1 reshape.112
  264.1 0.1 slice.12
  264.2 0.2 reshape.123
  264.4 3.5 fusion.54
  267.9 36.3 %pmax.7 = f32[8,2,8,5]{3,1,2,0:T(2,128)S(1)} all-reduce(f32[8,2,8,5]{3,1,2,0:T(2,128)S(1)} %get-tuple-element.48), channel_id=1, replica_groups=mesh['dp'=4,'tp'=8] {'tp'}, use_global_device_ids=true, to_apply=%region_3.4 | all-reduce | flops 640 | bytes 5120 | tf_op jit(solution)/shard_map/pmax | solution.py:106
  304.2 1.3 fusion.55
  305.5 0.5 fusion.36
  306.0 3.9 fusion.23
  309.8 0.0 all-reduce.5.cloned.1.call-update
  309.9 0.0 all-gather.5.cloned.1.call-start
  309.9 0.0 all-to-all-done.1
  309.9 0.0 copy-start.2
  309.9 1.2 copy-done.2
  311.1 0.0 all-gather.5.cloned.1.call-update
  311.1 33.7 %psum.23 = f32[8,2,8,5]{3,1,2,0:T(2,128)S(1)} all-reduce(f32[8,2,8,5]{3,1,2,0:T(2,128)S(1)} %bitcast.105), channel_id=1, replica_groups=mesh['dp'=4,'tp'=8] {'tp'}, use_global_device_ids=true, to_apply=%region_7.8 | all-reduce | flops 640 | bytes 5120 | tf_op jit(solution)/shard_map/psum | solution.py:108
  344.8 0.3 fusion.44
  345.2 33.9 %all-reduce.5.cloned.1.call-done = f32[8,2,8,5,128]{4,3,1,2,0:T(8,128)} async-done(((f32[8,2,8,5,128]{4,3,1,2,0:T(8,128)}), f32[8,2,8,5,128]{4,3,1,2,0:T(8,128)}) %all-reduce.5.cloned.1.call-update) | async-done | bytes 327696 | tf_op jit(solution)/shard_map/psum | solution.py:108
  379.1 1.6 fusion.27
  380.6 0.1 copy.59
  380.7 0.2 convert_element_type.36
  380.9 0.0 all-gather.5.cloned.1.call-done
  381.0 3.8 fusion.33
  384.8 0.6 copy.61
  (7 shorter events, 0.1 us)
Async XLA Ops:
  18.9 8.9 %copy-start.5 = (s32[32,2]{0,1:T(2,128)S(1)}, s32[32,2]{0,1:T(2,128)}, u32[]{:S(2)}) copy-start(s32[32,2]{0,1:T(2,128)} %param.27) | copy-start | bytes 772
  20.5 65.0 %all-to-all-start = ((bf16[160,8,896]{2,0,1:T(8,128)(2,1)}), bf16[160,8,896]{2,0,1:T(8,128)(2,1)S(1)}, u32[]{:S(2)}, u32[]{:S(2)}) async-start(bf16[160,8,896]{2,0,1:T(8,128)(2,1)} %bitcast.93), calls=%async_computation | async-start | bytes 4587520 | tf_op jit(solution)/shard_map/all_to_all | solution.py:56
  27.8 197.9 %all-reduce.3.cloned.1.call-start = ((), (), s32[]{:S(2)}) async-start(), calls=%async_computation.2 | async-start | bytes 2621440 | tf_op jit(solution)/shard_map/psum | solution.py:74
  44.9 183.2 %all-gather.3.cloned.1.call-start = ((), (), s32[]{:S(2)}) async-start(), calls=%async_computation.3 | async-start | bytes 11468800 | tf_op jit(solution)/shard_map/all_gather | solution.py:60
  85.5 1.4 copy-start.1
  96.4 213.5 %all-to-all-start.1 = ((bf16[160,8,640]{2,0,1:T(8,128)(2,1)}), bf16[160,8,640]{2,0,1:T(8,128)(2,1)S(1)}, u32[]{:S(2)}, u32[]{:S(2)}) async-start(bf16[160,8,640]{2,0,1:T(8,128)(2,1)} %bitcast.74), calls=%async_computation.1 | async-start | bytes 3276800 | tf_op jit(solution)/shard_map/all_to_all | solution.py:57
  100.9 278.2 %all-reduce.5.cloned.1.call-start = ((), (), s32[]{:S(2)}) async-start(), calls=%async_computation.4 | async-start | bytes 1048576 | tf_op jit(solution)/shard_map/psum | solution.py:108
  100.9 5.5 %copy-start.3 = (bf16[8,256,1024]{2,1,0:T(8,128)(2,1)S(1)}, bf16[8,256,1024]{2,1,0:T(8,128)(2,1)}, u32[]{:S(2)}) copy-start(bf16[8,256,1024]{2,1,0:T(8,128)(2,1)} %param.25) | copy-start | bytes 12582916
  106.4 3.0 copy-start.6
  109.5 4.7 %copy-start = (bf16[256,8,8,128]{3,2,1,0:T(8,128)(2,1)S(1)}, bf16[256,8,8,128]{3,2,1,0:T(8,128)(2,1)}, u32[]{:S(2)}) copy-start(bf16[256,8,8,128]{3,2,1,0:T(8,128)(2,1)} %copy.76) | copy-start | bytes 12582916
  114.2 112.6 %copy-start.4 = (f32[5120]{0:T(1024)S(1)}, f32[5120]{0:T(1024)}, u32[]{:S(2)}) copy-start(f32[5120]{0:T(1024)} %param.22) | copy-start | bytes 61444
  309.9 71.1 %all-gather.5.cloned.1.call-start = ((), (), s32[]{:S(2)}) async-start(), calls=%async_computation.5 | async-start | bytes 8192000 | tf_op jit(solution)/shard_map/all_gather | solution.py:61
  309.9 1.2 copy-start.2
Sparse Core Ops, SparseCore 0:
  45.1 180.5 all-reduce.2
  310.0 69.0 all-reduce.4
Sparse Core Ops, SparseCore 1:
  87.1 62.7 all-gather.2
  312.0 44.2 all-gather.4
where the time goes:
time: 393 us
  waiting for transfers between devices  184 us (47%)
  blocking collectives  101 us (26%)
  matrix products  30 us (8%)
  local copies, waits for them, and re-layouts  28.4 us (7%)
  other arithmetic  22.1 us (6%)
  between operations  15.7 us (4%)
  starting transfers between devices  11.9 us (3%)
    psum x1, waiting for transfers between devices, on_device(): every_row = lax.psum(partial_rows, ('dp', 'tp'))  109 us
    all_to_all x1, waiting for transfers between devices, on_device(): lax.all_to_all(qkv_half, 'tp', split_axis=1, concat_axis=0, tiled=True)  40.5 us
    pmax x1, blocking collectives, on_device(): cache_top = lax.pmax(local_top, 'tp')  36.3 us
    psum x1, waiting for transfers between devices, on_device(): lax.psum((local_total * rescale, local_weighted * rescale[..., None]), 'tp')  33.9 us
    psum x1, blocking collectives, on_device(): lax.psum((local_total * rescale, local_weighted * rescale[..., None]), 'tp')  33.7 us
    all_gather x1, blocking collectives, on_device(): lax.all_gather(proj_part, 'tp', axis=1, tiled=True)  30.9 us
    unnamed x17, local copies, waits for them, and re-layouts  11.7 us
    dot_general x1, matrix products, on_device(): jnp.dot(selector, embed_table, preferred_element_type=jnp.float32)  11.1 us
  transfers between devices with their start and end apart: 6, of which 3 were waited for; matrix products, arithmetic and copies ran while one was open for 16% of the time, Pallas kernels for 0%

commit v1 on v0

--- a/solution.py
+++ b/solution.py
@@ -1,11 +1,17 @@
+import functools
+
 import jax
 import jax.numpy as jnp
 from jax import lax
+from jax.experimental import pallas as pl
+from jax.experimental.pallas import tpu as pltpu
 from jax.sharding import PartitionSpec as P
 
 HEADS = 40
 KV_HEADS = 8
 HEAD = 128
+GROUP = HEADS // KV_HEADS
+STEPS = 2
 
 
 BETA_ONE = 0.9
@@ -17,6 +23,10 @@
 CORR_ONE = 1.0 - 0.9**10
 CORR_TWO = 1.0 - 0.95**10
 MASK_LOW = -1e30
+BOTH = ("dp", "tp")
+F32 = jnp.float32
+BF16 = jnp.bfloat16
+VMEM_LIMIT = 48 * 1024 * 1024
 
 
 def adamw(master, first, second, grad):
@@ -28,7 +38,370 @@
     return (master_new, first_new, second_new)
 
 
-def on_device(
+def lookup_kernel(dp, tp, ids_ref, table_ref, tail_ref, gain_ref, keep_ref, send_ref, own_ref,
+                  buf, raw, nrm, sems):
+    tokens, width = raw.shape
+    vocab_rows = table_ref.shape[0]
+    whole = vocab_rows // 16 * 16
+    depth = width // (dp * tp)
+    my_dp = lax.axis_index("dp")
+    base = (my_dp * tp + lax.axis_index("tp")) * vocab_rows
+
+    def local(t):
+        return ids_ref[t // STEPS, t % STEPS] - base
+
+    def owned(t):
+        entry = local(t)
+        return jnp.logical_and(entry >= 0, entry < vocab_rows)
+
+    def fetch(t, _):
+        entry = local(t)
+        mine = owned(t)
+
+        @pl.when(jnp.logical_and(mine, entry < whole))
+        def _():
+            start = pl.multiple_of(entry // 16 * 16, 16)
+            pltpu.make_async_copy(table_ref.at[pl.ds(start, 16)], buf.at[t], sems.at[t]).start()
+
+        @pl.when(jnp.logical_and(mine, entry >= whole))
+        def _():
+            pltpu.make_async_copy(tail_ref, buf.at[t], sems.at[t]).start()
+
+        return 0
+
+    lax.fori_loop(0, tokens, fetch, 0)
+    raw[...] = jnp.zeros_like(raw)
+    nrm[...] = jnp.zeros_like(nrm)
+
+    def take(t, _):
+        entry = local(t)
+
+        @pl.when(owned(t))
+        def _():
+            pltpu.make_async_copy(tail_ref, buf.at[t], sems.at[t]).wait()
+            at = jnp.where(entry < whole, entry % 16, entry - (vocab_rows - 16))
+            picked = lax.broadcasted_iota(jnp.int32, (16, width), 0) == at
+            row = jnp.sum(
+                jnp.where(picked, buf[t].astype(F32), 0.0), axis=0, keepdims=True
+            )
+            meansq = jnp.mean(row * row, axis=-1, keepdims=True)
+            raw[pl.ds(t, 1), :] = row
+            nrm[pl.ds(t, 1), :] = row * lax.rsqrt(meansq + EPS_NORM) * gain_ref[...]
+
+        return 0
+
+    lax.fori_loop(0, tokens, take, 0)
+    own_ref[...] = raw[...].astype(BF16)
+    quarter = tokens // 4
+
+    def block(b):
+        main = nrm[:, depth * b : depth * b + 128]
+        rest = nrm[:, depth * b + 128 : depth * (b + 1)]
+        rest = jnp.concatenate(
+            [rest[quarter * i : quarter * (i + 1)] for i in range(4)], axis=1
+        )
+        return jnp.concatenate([main, rest], axis=0)
+
+    even = my_dp % 2 == 0
+    for x in range(dp // 2):
+        for t in range(tp):
+            at_even = block((2 * x) * tp + t)
+            at_odd = block((2 * x + 1) * tp + t)
+            keep_ref[x * tp + t] = jnp.where(even, at_even, at_odd).astype(BF16)
+            send_ref[x * tp + t] = jnp.where(even, at_odd, at_even).astype(BF16)
+
+
+def by_core(rows, dp, per_dp):
+    even = lax.axis_index("dp") % 2 == 0
+    mine, other = [], []
+    for x in range(dp // 2):
+        at_even = rows[(2 * x) * per_dp : (2 * x + 1) * per_dp]
+        at_odd = rows[(2 * x + 1) * per_dp : (2 * x + 2) * per_dp]
+        mine.append(jnp.where(even, at_even, at_odd))
+        other.append(jnp.where(even, at_odd, at_even))
+    return jnp.concatenate(mine + other, axis=0)
+
+
+def project_kernel(dp, tp, blocks_ref, weight_ref, keep_ref, send_ref):
+    tokens = 64
+    per_dp = tokens // dp
+    quarter = tokens // 4
+    width = HEADS * HEAD
+    kv_width = KV_HEADS * HEAD
+    total = jnp.sum(blocks_ref[...].astype(F32), axis=0)
+    main = by_core(total[:tokens], dp, per_dp).astype(BF16)
+    rest = total[tokens:]
+    rest = jnp.concatenate([rest[:, 32 * i : 32 * (i + 1)] for i in range(4)], axis=0)
+    rest = by_core(rest, dp, per_dp).astype(BF16)
+    half = tokens // 2
+
+    def dot(at, size):
+        return jnp.dot(
+            main, weight_ref[0:128, at : at + size], preferred_element_type=F32
+        ) + jnp.dot(rest, weight_ref[128:160, at : at + size], preferred_element_type=F32)
+
+    for g in range(tp):
+        spans = (
+            (0, g * GROUP * HEAD, GROUP * HEAD),
+            (GROUP * HEAD, width + g * HEAD, HEAD),
+            ((GROUP + 1) * HEAD, width + kv_width + g * HEAD, HEAD),
+        )
+        for to, at, size in spans:
+            part = dot(at, size)
+            for x in range(dp // 2):
+                keep_ref[x * tp + g, :, to : to + size] = part[per_dp * x : per_dp * (x + 1)]
+                send_ref[x * tp + g, :, to : to + size] = part[
+                    half + per_dp * x : half + per_dp * (x + 1)
+                ]
+
+
+def attend_kernel(dp, tp, lengths_ref, qkv_ref, keys_ref, values_ref, msg_ref, joined, level):
+    g = pl.program_id(0)
+    rows, span = keys_ref.shape[0], keys_ref.shape[1]
+    per_dp = rows * STEPS
+    lines = GROUP * per_dp
+    my_tp = lax.axis_index("tp")
+    depth = HEADS * HEAD // (dp * tp)
+    scale = HEAD ** (-0.5)
+
+    packed = qkv_ref[0]
+    queries = jnp.concatenate(
+        [packed[:, HEAD * h : HEAD * (h + 1)] for h in range(GROUP)], axis=0
+    )
+    fresh_keys = packed[:, GROUP * HEAD : (GROUP + 1) * HEAD]
+    fresh_values = packed[:, (GROUP + 1) * HEAD :]
+    nt = (((1,), (1,)), ((), ()))
+
+    line = lax.broadcasted_iota(jnp.int32, (lines, 1), 0) % per_dp
+    row_of = line // STEPS
+    length = jnp.zeros((lines, 1), jnp.int32)
+    scores = jnp.zeros((lines, span), F32)
+    for r in range(rows):
+        length = jnp.where(row_of == r, lengths_ref[r], length)
+        part = lax.dot_general(queries, keys_ref[r], nt, preferred_element_type=F32)
+        scores = jnp.where(row_of == r, part, scores)
+    position = my_tp * span + lax.broadcasted_iota(jnp.int32, (lines, span), 1)
+    live = position < length
+    scores = jnp.where(live, scores * scale, MASK_LOW)
+
+    column = lax.broadcasted_iota(jnp.int32, (lines, per_dp), 1)
+    fresh = lax.dot_general(queries, fresh_keys, nt, preferred_element_type=F32) * scale
+    seen = (column // STEPS == row_of) & (column <= line) & (my_tp == g)
+    fresh = jnp.where(seen, fresh, MASK_LOW)
+
+    top = jnp.maximum(
+        jnp.max(scores, axis=-1, keepdims=True), jnp.max(fresh, axis=-1, keepdims=True)
+    )
+    probs = jnp.where(live, jnp.exp(scores - top), 0.0)
+    fresh_probs = jnp.where(seen, jnp.exp(fresh - top), 0.0)
+    total = jnp.sum(probs, axis=-1, keepdims=True) + jnp.sum(fresh_probs, axis=-1, keepdims=True)
+    weighted = jnp.dot(fresh_probs.astype(BF16), fresh_values, preferred_element_type=F32)
+    probs = probs.astype(BF16)
+    for r in range(rows):
+        weighted += jnp.dot(
+            jnp.where(row_of == r, probs, jnp.zeros_like(probs)),
+            values_ref[r],
+            preferred_element_type=F32,
+        )
+    some = total > 0.0
+    safe = jnp.where(some, total, 1.0)
+    outcome = weighted / safe
+    logsum = jnp.where(some, top + jnp.log(safe), MASK_LOW)
+    lane = lax.broadcasted_iota(jnp.int32, (per_dp, HEAD), 1)
+    levels = level[...]
+    for h in range(GROUP):
+        at = pl.multiple_of((g * GROUP + h) * HEAD, HEAD)
+        joined[:, pl.ds(at, HEAD)] = outcome[per_dp * h : per_dp * (h + 1)]
+        levels = jnp.where(
+            lane == g * GROUP + h, logsum[per_dp * h : per_dp * (h + 1)], levels
+        )
+    level[...] = levels
+
+    @pl.when(g == KV_HEADS - 1)
+    def _():
+        final = level[...]
+        high = final.astype(BF16).astype(F32)
+        middle = (final - high).astype(BF16).astype(F32)
+        low = final - high - middle
+        for b in range(dp * tp):
+            h = depth * b // HEAD
+            pieces = [joined[:, depth * b : depth * (b + 1)]]
+            for head in (h, h + 1):
+                for part in (high, middle, low):
+                    pieces.append(part[:, head : head + 1])
+            pieces.append(jnp.zeros((per_dp, 256 - depth - 6), F32))
+            msg_ref[b] = jnp.concatenate(pieces, axis=1).astype(BF16)
+
+
+def output_kernel(dp, tp, msg_ref, weight_ref, own_ref, keep_ref, send_ref):
+    depth = weight_ref.shape[0]
+    per_dp = msg_ref.shape[1]
+    my_block = lax.axis_index("dp") * tp + lax.axis_index("tp")
+    edge = HEAD - (depth * my_block) % HEAD
+    first_head = lax.broadcasted_iota(jnp.int32, (per_dp, depth), 1) < edge
+    merged = []
+    for d in range(dp):
+        parts, levels = [], []
+        for t in range(tp):
+            block = msg_ref[d * tp + t].astype(F32)
+            stats = [block[:, depth + i : depth + i + 1] for i in range(6)]
+            one = stats[0] + stats[1] + stats[2]
+            two = stats[3] + stats[4] + stats[5]
+            levels.append(jnp.where(first_head, one, two))
+            parts.append(block[:, :depth])
+        top = functools.reduce(jnp.maximum, levels)
+        total = jnp.zeros_like(top)
+        weighted = jnp.zeros_like(top)
+        for part, lev in zip(parts, levels):
+            share = jnp.exp(lev - top)
+            total += share
+            weighted += share * part
+        merged.append(weighted / total)
+    attended = by_core(jnp.concatenate(merged, axis=0), dp, per_dp).astype(BF16)
+    half = dp // 2 * per_dp
+    out_width = weight_ref.shape[1] // tp
+    for t in range(tp):
+        cols = slice(out_width * t, out_width * (t + 1))
+        part = jnp.dot(attended, weight_ref[:, cols], preferred_element_type=F32)
+        part += by_core(own_ref[:, cols].astype(F32), dp, per_dp)
+        for x in range(dp // 2):
+            keep_ref[x * tp + t] = part[per_dp * x : per_dp * (x + 1)]
+            send_ref[x * tp + t] = part[half + per_dp * x : half + per_dp * (x + 1)]
+
+
+def whole(shape_count):
+    return [pl.BlockSpec(memory_space=pltpu.VMEM)] * shape_count
+
+
+def on_device_partial(
+    dp,
+    tp,
+    qkv_master,
+    qkv_first,
+    qkv_second,
+    qkv_grad,
+    out_master,
+    out_first,
+    out_second,
+    out_grad,
+    norm_gain,
+    embed_table,
+    cache_keys,
+    cache_values,
+    cache_lengths,
+    token_ids,
+):
+    width = embed_table.shape[1]
+    group_rows, span = cache_keys.shape[0], cache_keys.shape[1]
+    per_dp = group_rows * STEPS
+    tokens = per_dp * dp
+    half = dp // 2 * tp
+    depth = width // (dp * tp)
+    packed = width // (dp * tp) * tokens // 128
+    out_width = width // tp
+    joined_width = (GROUP + 2) * HEAD
+    params = pltpu.CompilerParams(vmem_limit_bytes=VMEM_LIMIT)
+
+    core_pairs = [
+        (d * tp + t, (d ^ 1) * tp + t) for d in range(dp) for t in range(tp)
+    ]
+    same_core = [
+        [(2 * x + c) * tp + t for x in range(dp // 2) for t in range(tp)] for c in range(2)
+    ]
+
+    def other_core(value):
+        return lax.ppermute(value, BOTH, core_pairs)
+
+    def among_chips(value):
+        return lax.all_to_all(value, BOTH, 0, 0, tiled=True, axis_index_groups=same_core)
+
+    keep, send, own_rows = pl.pallas_call(
+        functools.partial(lookup_kernel, dp, tp),
+        out_shape=(
+            jax.ShapeDtypeStruct((half, packed, 128), BF16),
+            jax.ShapeDtypeStruct((half, packed, 128), BF16),
+            jax.ShapeDtypeStruct((tokens, width), BF16),
+        ),
+        in_specs=[
+            pl.BlockSpec(memory_space=pltpu.SMEM),
+            pl.BlockSpec(memory_space=pl.ANY),
+            pl.BlockSpec(memory_space=pl.ANY),
+            pl.BlockSpec(memory_space=pltpu.VMEM),
+        ],
+        out_specs=tuple(whole(3)),
+        scratch_shapes=[
+            pltpu.VMEM((tokens, 16, width), BF16),
+            pltpu.VMEM((tokens, width), F32),
+            pltpu.VMEM((tokens, width), F32),
+            pltpu.SemaphoreType.DMA((tokens,)),
+        ],
+        compiler_params=params,
+        name="lookup",
+    )(token_ids, embed_table, embed_table[-16:], norm_gain.reshape(1, width))
+    blocks = among_chips(keep + other_core(send))
+
+    qkv_master_new, qkv_first_new, qkv_second_new = adamw(
+        qkv_master, qkv_first, qkv_second, qkv_grad
+    )
+    out_master_new, out_first_new, out_second_new = adamw(
+        out_master, out_first, out_second, out_grad
+    )
+    qkv_half = qkv_master_new.astype(BF16)
+    out_half = out_master_new.astype(BF16)
+
+    keep, send = pl.pallas_call(
+        functools.partial(project_kernel, dp, tp),
+        out_shape=(jax.ShapeDtypeStruct((half, per_dp, joined_width), F32),) * 2,
+        in_specs=whole(2),
+        out_specs=tuple(whole(2)),
+        compiler_params=params,
+        name="project",
+    )(blocks, qkv_half)
+    partial = among_chips(keep + other_core(send))
+    projected = jnp.sum(partial, axis=0).astype(BF16)
+    joined = lax.all_to_all(
+        jnp.broadcast_to(projected[None], (tp,) + projected.shape), "tp", 0, 0, tiled=True
+    )
+
+    messages = pl.pallas_call(
+        functools.partial(attend_kernel, dp, tp),
+        grid=(KV_HEADS,),
+        out_shape=jax.ShapeDtypeStruct((dp * tp, per_dp, 256), BF16),
+        in_specs=[
+            pl.BlockSpec(memory_space=pltpu.SMEM),
+            pl.BlockSpec((1, per_dp, joined_width), lambda g: (g, 0, 0)),
+            pl.BlockSpec((group_rows, span, HEAD), lambda g: (0, 0, g)),
+            pl.BlockSpec((group_rows, span, HEAD), lambda g: (0, 0, g)),
+        ],
+        out_specs=pl.BlockSpec((dp * tp, per_dp, 256), lambda g: (0, 0, 0)),
+        scratch_shapes=[pltpu.VMEM((per_dp, width), F32), pltpu.VMEM((per_dp, HEAD), F32)],
+        compiler_params=params,
+        name="attend",
+    )(cache_lengths, joined, cache_keys, cache_values)
+    arrived = lax.all_to_all(messages, BOTH, 0, 0, tiled=True)
+
+    keep, send = pl.pallas_call(
+        functools.partial(output_kernel, dp, tp),
+        out_shape=(jax.ShapeDtypeStruct((half, per_dp, out_width), F32),) * 2,
+        in_specs=whole(3),
+        out_specs=tuple(whole(2)),
+        compiler_params=params,
+        name="output",
+    )(arrived, out_half, own_rows)
+    sums = among_chips((keep + other_core(send)).astype(BF16))
+    layer_out = jnp.sum(sums.astype(F32), axis=0).astype(BF16)
+    return (
+        qkv_master_new,
+        qkv_first_new,
+        qkv_second_new,
+        out_master_new,
+        out_first_new,
+        out_second_new,
+        layer_out.reshape(group_rows, STEPS, out_width),
+    )
+
+
+def on_device_general(
     qkv_master,
     qkv_first,
     qkv_second,
@@ -144,6 +517,7 @@
 
 
 def solution(mesh):
+    dp, tp = mesh.shape["dp"], mesh.shape["tp"]
     placed = (
         P(("dp", "tp"), None),
         P(("dp", "tp"), None),
@@ -160,8 +534,11 @@
         P("dp"),
         P(),
     )
+    body = on_device_general
+    if (dp, tp) == (4, KV_HEADS):
+        body = functools.partial(on_device_partial, dp, tp)
     return jax.shard_map(
-        on_device,
+        body,
         mesh=mesh,
         in_specs=placed,
         out_specs=(

time: 393 us -> 122 us (0.31)
  waiting for transfers between devices: 184 us -> 9.26 us
  blocking collectives: 101 us -> 56.9 us
  matrix products: 30 us -> 0 us
  local copies, waits for them, and re-layouts: 28.4 us -> 5.26 us
  Pallas kernels: 0 us -> 17.8 us
  between operations: 15.7 us -> 0.72 us
    psum x2 -> x0, waiting for transfers between devices: 143 us -> none  [the longest x1 109 us: on_device(): every_row = lax.psum(partial_rows, ('dp', 'tp'))]
    all_to_all x0 -> x3, blocking collectives: none -> 56.9 us  [the longest x2 45.8 us: among_chips(): lax.all_to_all(value, BOTH, 0, 0, tiled=True, axis_index_groups=same_core)]
    all_to_all x2, waiting for transfers between devices: 40.5 us -> 3.36 us  [the longest x1 2.67 us: on_device_partial(): arrived = lax.all_to_all(messages, BOTH, 0, 0, tiled=True)]
    pmax x1 -> x0, blocking collectives: 36.3 us -> none  [on_device(): cache_top = lax.pmax(local_top, 'tp')]
    psum x1 -> x0, blocking collectives: 33.7 us -> none  [on_device(): lax.psum((local_total * rescale, local_weighted * rescale[..., None]), 'tp')]
    all_gather x1 -> x0, blocking collectives: 30.9 us -> none  [on_device(): lax.all_gather(proj_part, 'tp', axis=1, tiled=True)]
    dot_general x7 -> x0, matrix products: 30 us -> none  [the longest x1 11.1 us: on_device(): jnp.dot(selector, embed_table, preferred_element_type=jnp.float32)]
    pallas_call x0 -> x4, Pallas kernels: none -> 17.8 us  [the longest x1 9.26 us: on_device_partial(): pl.pallas_call(functools.partial(attend_kernel, dp, tp), grid=(KV_HEADS,)...]
  transfers between devices with their start and end apart: 6 -> 5, of which waited for: 3 -> 5; matrix products, arithmetic and copies ran while one was open for 16% -> 16% of each run, Pallas kernels for 0% -> 0%
where the time goes in v1:
time: 122 us; the launch traced here: 121 us
  blocking collectives  56.9 us (47%)
  other arithmetic  20 us (16%)
  Pallas kernels  17.8 us (15%)
  starting transfers between devices  11.6 us (10%)
  waiting for transfers between devices  9.26 us (8%)
  local copies, waits for them, and re-layouts  5.26 us (4%)
    all_to_all x2, blocking collectives, among_chips(): lax.all_to_all(value, BOTH, 0, 0, tiled=True, axis_index_groups=same_core)  45.8 us
    all_to_all x1, blocking collectives, on_device_partial(): lax.all_to_all(jnp.broadcast_to(projected[None], (tp,) + projected.shape)...  11.1 us
    convert_element_type x1, other arithmetic, on_device_partial(): qkv_half = qkv_master_new.astype(BF16)  10.9 us
    pallas_call x1, Pallas kernels, on_device_partial(): pl.pallas_call(functools.partial(attend_kernel, dp, tp), grid=(KV_HEADS,)...  9.26 us
    all_to_all x1, starting transfers between devices, among_chips(): lax.all_to_all(value, BOTH, 0, 0, tiled=True, axis_index_groups=same_core)  8.5 us
    convert_element_type x1, other arithmetic, on_device_partial(): out_half = out_master_new.astype(BF16)  7.97 us
    pallas_call x1, Pallas kernels, on_device_partial(): pl.pallas_call(functools.partial(lookup_kernel, dp, tp), out_shape=(jax.S...  6.91 us
    ppermute x3, waiting for transfers between devices, other_core(): return lax.ppermute(value, BOTH, core_pairs)  5.91 us
  transfers between devices with their start and end apart: 5, of which 5 were waited for; matrix products, arithmetic and copies ran while one was open for 16% of the time, Pallas kernels for 0%

profile of v1, /device:TPU:0, one launch (start us, length us, event | category | flops | bytes accessed | tf_op | source)
XLA Modules:
  0.0 121.4 jit_solution(13681619834153069269)
XLA Ops:
  0.6 0.9 slice.3.tail_ref
  1.6 0.8 copy.21.ids_ref
  2.3 0.0 copy-start.1
  2.3 0.7 copy-done.1
  3.1 6.9 %lookup.1 = (bf16[16,80,128]{2,1,0:T(8,128)(2,1)S(1)}, bf16[16,80,128]{2,1,0:T(8,128)(2,1)S(1)}, bf16[64,5120]{1,0:T(8,128)(2,1)S(1)}) custom-call(s32[32,2]{1,0:T(8,128)S(1)} %copy.21.ids_ref, bf16[2376,5120]{1,0:T(8,128)(2,1)} %table_ref.1, bf16[16,5120]{1,0:T(8,128)(2,1)S(1)} %slice.3.tail_ref, f32[1,5120]{1,0:T(1,128)S(1)} %bitcast.1), custom_call_target="tpu_custom_call" | custom-call | tf_op jit(solution)/shard_map/lookup/pallas_call | solution.py:318
  10.0 0.3 collective-permute-start
  10.3 1.4 %collective-permute-done = bf16[16,80,128]{2,1,0:T(8,128)(2,1)S(1)} collective-permute-done((bf16[16,80,128]{2,1,0:T(8,128)(2,1)S(1)}, bf16[16,80,128]{2,1,0:T(8,128)(2,1)S(1)}, u32[]{:S(2)}, u32[]{:S(2)}) %collective-permute-start) | collective-permute-done | bytes 327712 | tf_op jit(solution)/shard_map/ppermute | solution.py:313
  11.7 0.8 add.49
  12.5 8.5 %all-to-all-start = ((bf16[16,80,128]{2,1,0:T(8,128)(2,1)}), bf16[16,80,128]{2,1,0:T(8,128)(2,1)S(1)}, u32[]{:S(2)}, u32[]{:S(2)}) async-start(bf16[16,80,128]{2,1,0:T(8,128)(2,1)} %add.49), calls=%async_computation | async-start | bytes 655360 | tf_op jit(solution)/shard_map/all_to_all | solution.py:316
  21.0 10.9 %fusion.7 = (bf16[160,7168]{1,0:T(8,128)(2,1)S(1)}, f32[160,7168]{1,0:T(8,128)}, f32[160,7168]{1,0:T(8,128)}, f32[160,7168]{1,0:T(8,128)}) fusion(f32[160,7168]{1,0:T(8,128)} %param.14, bf16[160,7168]{1,0:T(8,128)(2,1)} %param.17, f32[160,7168]{1,0:T(8,128)} %param.15, f32[160,7168]{1,0:T(8,128)} %param.16), kind=kLoop, calls=%fused_computation.12 | loop fusion | flops 19496960 | bytes 32112640 | tf_op jit(solution)/shard_map/convert_element_type | solution.py:349
  31.9 0.7 all-to-all-done.blocks_ref
  32.6 0.8 project.1
  33.4 0.0 copy-start.2
  33.4 0.1 collective-permute-start.1
  33.5 2.5 %collective-permute-done.1 = f32[16,16,896]{2,1,0:T(8,128)S(1)} collective-permute-done((f32[16,16,896]{2,1,0:T(8,128)S(1)}, f32[16,16,896]{2,1,0:T(8,128)S(1)}, u32[]{:S(2)}, u32[]{:S(2)}) %collective-permute-start.1) | collective-permute-done | bytes 917536 | tf_op jit(solution)/shard_map/ppermute | solution.py:313
  36.0 0.1 add.50
  36.1 30.2 %all_to_all.25 = f32[16,16,896]{2,1,0:T(8,128)S(1)} all-to-all(f32[16,16,896]{2,1,0:T(8,128)S(1)} %add.50), channel_id=1, replica_groups={{0,1,2,3,4,5,6,7,16,17,18,19,20,21,22,23},{8,9,10,11,12,13,14,15,24,25,..., dimensions={0} | all-to-all | bytes 1835008 | tf_op jit(solution)/shard_map/all_to_all | solution.py:316
  66.2 0.1 reduce_sum.21
  66.3 11.1 %all_to_all.26.qkv_ref = bf16[8,16,896]{2,1,0:T(8,128)(2,1)S(1)} all-to-all(bf16[8,16,896]{2,1,0:T(8,128)(2,1)S(1)} %broadcast_in_dim.2), channel_id=1, replica_groups=mesh['dp'=4,'tp'=8] {'tp'}, dimensions={0} | all-to-all | bytes 458752 | tf_op jit(solution)/shard_map/all_to_all | solution.py:362
  77.4 0.0 copy-done.2
  77.4 0.0 copy-start
  77.4 2.2 %copy-done = bf16[8,256,1024]{2,1,0:T(8,128)(2,1)S(1)} copy-done((bf16[8,256,1024]{2,1,0:T(8,128)(2,1)S(1)}, bf16[8,256,1024]{2,1,0:T(8,128)(2,1)}, u32[]{:S(2)}) %copy-start) | copy-done | bytes 4194328
  79.6 9.3 %attend.1 = bf16[32,16,256]{2,1,0:T(8,128)(2,1)} custom-call(s32[8]{0:T(128)S(1)} %copy-done.2, bf16[8,16,896]{2,1,0:T(8,128)(2,1)S(1)} %all_to_all.26.qkv_ref, bf16[8,256,1024]{2,1,0:T(8,128)(2,1)S(1)} %copy-done, bf16[8,256,1024]{2,1,0:T(8,128)(2,1)} %values_ref.1), custom_call_target="tpu_custom_call" | custom-call | tf_op jit(solution)/shard_map/attend/pallas_call | solution.py:366
  88.8 2.6 %all-to-all-start.3 = ((bf16[32,16,256]{2,1,0:T(8,128)(2,1)}), bf16[32,16,256]{2,1,0:T(8,128)(2,1)S(1)}, u32[]{:S(2)}, u32[]{:S(2)}) async-start(bf16[32,16,256]{2,1,0:T(8,128)(2,1)} %attend.1), calls=%async_computation.3 | async-start | bytes 524288 | tf_op jit(solution)/shard_map/all_to_all | solution.py:381
  91.4 8.0 %fusion.4 = (bf16[160,5120]{1,0:T(8,128)(2,1)S(1)}, f32[160,5120]{1,0:T(8,128)}, f32[160,5120]{1,0:T(8,128)}, f32[160,5120]{1,0:T(8,128)}) fusion(f32[160,5120]{1,0:T(8,128)} %param.18, bf16[160,5120]{1,0:T(8,128)(2,1)} %param.21, f32[160,5120]{1,0:T(8,128)} %param.19, f32[160,5120]{1,0:T(8,128)} %param.20), kind=kLoop, calls=%fused_computation.11 | loop fusion | flops 13926400 | bytes 22937600 | tf_op jit(solution)/shard_map/convert_element_type | solution.py:350
  99.4 2.7 %all-to-all-done.3.msg_ref = bf16[32,16,256]{2,1,0:T(8,128)(2,1)S(1)} async-done(((bf16[32,16,256]{2,1,0:T(8,128)(2,1)}), bf16[32,16,256]{2,1,0:T(8,128)(2,1)S(1)}, u32[]{:S(2)}, u32[]{:S(2)}) %all-to-all-start.3) | async-done | bytes 262176 | tf_op jit(solution)/shard_map/all_to_all | solution.py:381
  102.1 0.8 output.1
  102.9 0.1 collective-permute-start.2
  102.9 2.1 %collective-permute-done.2 = f32[16,16,640]{2,1,0:T(8,128)S(1)} collective-permute-done((f32[16,16,640]{2,1,0:T(8,128)S(1)}, f32[16,16,640]{2,1,0:T(8,128)S(1)}, u32[]{:S(2)}, u32[]{:S(2)}) %collective-permute-start.2) | collective-permute-done | bytes 655392 | tf_op jit(solution)/shard_map/ppermute | solution.py:313
  105.0 0.1 add_convert_fusion
  105.1 15.6 %all_to_all.27 = bf16[16,16,640]{2,1,0:T(8,128)(2,1)S(1)} all-to-all(bf16[16,16,640]{2,1,0:T(8,128)(2,1)S(1)} %add_convert_fusion), channel_id=1, replica_groups={{0,1,2,3,4,5,6,7,16,17,18,19,20,21,22,23},{8,9,10,11,12,13,14,15,24,25,..., dimensions={0} | all-to-all | bytes 655360 | tf_op jit(solution)/shard_map/all_to_all | solution.py:316
  120.7 0.1 reduce_sum.22
  120.8 0.6 reshape.24
  (1 shorter events, 0.0 us)
Async XLA Ops:
  2.3 0.7 copy-start.1
  10.0 1.7 %collective-permute-start = (bf16[16,80,128]{2,1,0:T(8,128)(2,1)S(1)}, bf16[16,80,128]{2,1,0:T(8,128)(2,1)S(1)}, u32[]{:S(2)}, u32[]{:S(2)}) collective-permute-start(bf16[16,80,128]{2,1,0:T(8,128)(2,1)S(1)} %get-tuple-element.15), channel_id=1, source_target_pairs={{0,8},{1,9},{2,10},{3,11},{4,12},{5,13},{6,14},{7,15},{8,0},{9,1},... | collective-permute-start | bytes 983048 | tf_op jit(solution)/shard_map/ppermute | solution.py:313
  12.5 20.1 %all-to-all-start = ((bf16[16,80,128]{2,1,0:T(8,128)(2,1)}), bf16[16,80,128]{2,1,0:T(8,128)(2,1)S(1)}, u32[]{:S(2)}, u32[]{:S(2)}) async-start(bf16[16,80,128]{2,1,0:T(8,128)(2,1)} %add.49), calls=%async_computation | async-start | bytes 655360 | tf_op jit(solution)/shard_map/all_to_all | solution.py:316
  33.4 44.0 %copy-start.2 = (s32[8]{0:T(128)S(1)}, s32[8]{0:T(128)}, u32[]{:S(2)}) copy-start(s32[8]{0:T(128)} %lengths_ref.1) | copy-start | bytes 100
  33.4 2.5 %collective-permute-start.1 = (f32[16,16,896]{2,1,0:T(8,128)S(1)}, f32[16,16,896]{2,1,0:T(8,128)S(1)}, u32[]{:S(2)}, u32[]{:S(2)}) collective-permute-start(f32[16,16,896]{2,1,0:T(8,128)S(1)} %get-tuple-element.17), channel_id=1, source_target_pairs={{0,8},{1,9},{2,10},{3,11},{4,12},{5,13},{6,14},{7,15},{8,0},{9,1},... | collective-permute-start | bytes 2752520 | tf_op jit(solution)/shard_map/ppermute | solution.py:313
  77.4 2.2 %copy-start = (bf16[8,256,1024]{2,1,0:T(8,128)(2,1)S(1)}, bf16[8,256,1024]{2,1,0:T(8,128)(2,1)}, u32[]{:S(2)}) copy-start(bf16[8,256,1024]{2,1,0:T(8,128)(2,1)} %keys_ref.1) | copy-start | bytes 12582916
  88.8 13.2 %all-to-all-start.3 = ((bf16[32,16,256]{2,1,0:T(8,128)(2,1)}), bf16[32,16,256]{2,1,0:T(8,128)(2,1)S(1)}, u32[]{:S(2)}, u32[]{:S(2)}) async-start(bf16[32,16,256]{2,1,0:T(8,128)(2,1)} %attend.1), calls=%async_computation.3 | async-start | bytes 524288 | tf_op jit(solution)/shard_map/all_to_all | solution.py:381
  102.9 2.2 %collective-permute-start.2 = (f32[16,16,640]{2,1,0:T(8,128)S(1)}, f32[16,16,640]{2,1,0:T(8,128)S(1)}, u32[]{:S(2)}, u32[]{:S(2)}) collective-permute-start(f32[16,16,640]{2,1,0:T(8,128)S(1)} %get-tuple-element.20), channel_id=1, source_target_pairs={{0,8},{1,9},{2,10},{3,11},{4,12},{5,13},{6,14},{7,15},{8,0},{9,1},... | collective-permute-start | bytes 1966088 | tf_op jit(solution)/shard_map/ppermute | solution.py:313

commit v2 on v1

--- a/solution.py
+++ b/solution.py
@@ -12,6 +12,7 @@
 HEAD = 128
 GROUP = HEADS // KV_HEADS
 STEPS = 2
+SLOTS = 8
 
 
 BETA_ONE = 0.9
@@ -26,7 +27,7 @@
 BOTH = ("dp", "tp")
 F32 = jnp.float32
 BF16 = jnp.bfloat16
-VMEM_LIMIT = 48 * 1024 * 1024
+MIB = 1024 * 1024
 
 
 def adamw(master, first, second, grad):
@@ -38,77 +39,134 @@
     return (master_new, first_new, second_new)
 
 
-def lookup_kernel(dp, tp, ids_ref, table_ref, tail_ref, gain_ref, keep_ref, send_ref, own_ref,
-                  buf, raw, nrm, sems):
+def lookup_kernel(dp, tp, ids_ref, table_ref, gain_ref, msg_ref, raw_ref, place_ref, most_ref,
+                  buf, gain, raw, column, entries, sems, gain_sem):
     tokens, width = raw.shape
+    per_dp = tokens // dp
     vocab_rows = table_ref.shape[0]
     whole = vocab_rows // 16 * 16
+    left = vocab_rows - whole
     depth = width // (dp * tp)
-    my_dp = lax.axis_index("dp")
-    base = (my_dp * tp + lax.axis_index("tp")) * vocab_rows
-
-    def local(t):
-        return ids_ref[t // STEPS, t % STEPS] - base
-
-    def owned(t):
-        entry = local(t)
-        return jnp.logical_and(entry >= 0, entry < vocab_rows)
-
-    def fetch(t, _):
-        entry = local(t)
-        mine = owned(t)
+    my_core = lax.axis_index("dp") % 2
+    base = (lax.axis_index("dp") * tp + lax.axis_index("tp")) * vocab_rows
+    gain_copy = pltpu.make_async_copy(gain_ref, gain, gain_sem)
+    gain_copy.start()
+
+    def whole_rows(entry, rank):
+        start = pl.multiple_of(entry // 16 * 16, 16)
+        return pltpu.make_async_copy(
+            table_ref.at[pl.ds(start, 16)], buf.at[rank], sems.at[rank]
+        )
+
+    def last_rows(rank):
+        return pltpu.make_async_copy(
+            table_ref.at[pl.ds(whole, left)], buf.at[rank, pl.ds(0, left)], sems.at[rank]
+        )
+
+    def fetch(t, held):
+        entry = ids_ref[t % STEPS, t // STEPS] - base
+        mine = jnp.logical_and(entry >= 0, entry < vocab_rows)
+        entries[held] = entry
 
         @pl.when(jnp.logical_and(mine, entry < whole))
         def _():
-            start = pl.multiple_of(entry // 16 * 16, 16)
-            pltpu.make_async_copy(table_ref.at[pl.ds(start, 16)], buf.at[t], sems.at[t]).start()
-
-        @pl.when(jnp.logical_and(mine, entry >= whole))
+            whole_rows(entry, held).start()
+
+        if left:
+            @pl.when(jnp.logical_and(mine, entry >= whole))
+            def _():
+                last_rows(held).start()
+
+        return held + mine.astype(jnp.int32)
+
+    buf[0:SLOTS] = jnp.zeros((SLOTS, 16, width), BF16)
+    held = lax.fori_loop(0, tokens, fetch, 0)
+    raw_ref[SLOTS:] = jnp.zeros((tokens - SLOTS, width), BF16)
+
+    def write(t, _):
+        group = t // per_dp
+        line = (group % 2 ^ my_core) * (tokens // 2) + group // 2 * per_dp + t % per_dp
+        column[pl.ds(line, 1), :] = jnp.full(
+            (1, 128), ids_ref[t % STEPS, t // STEPS], jnp.int32
+        )
+        return 0
+
+    lax.fori_loop(0, tokens, write, 0, unroll=8)
+    line = lax.broadcasted_iota(jnp.int32, (tokens, 128), 0)
+    inside = line % (tokens // 2)
+    order = (inside // per_dp * 2 + (line // (tokens // 2) ^ my_core)) * per_dp + line % per_dp
+    identity = column[...].astype(F32)
+    holder = jnp.floor(identity * (1.0 / vocab_rows))
+    holder = jnp.where(holder * vocab_rows > identity, holder - 1.0, holder)
+    holder = jnp.where((holder + 1.0) * vocab_rows <= identity, holder + 1.0, holder)
+    key = holder * tokens + order.astype(F32)
+    turned = jnp.transpose(
+        jnp.concatenate([key, jnp.full((128 - tokens, 128), -1.0, F32)], axis=0)
+    )[0:1, :]
+    before = (turned >= holder * tokens) & (turned < key)
+    rank = jnp.sum(before.astype(F32), axis=1, keepdims=True)
+    place_ref[...] = (holder * tokens + rank).astype(jnp.int32)
+    most_ref[0] = jnp.max(rank).astype(jnp.int32)
+
+    def arrive(rank):
+        entry = entries[rank]
+
+        @pl.when(entry < whole)
         def _():
-            pltpu.make_async_copy(tail_ref, buf.at[t], sems.at[t]).start()
-
-        return 0
-
-    lax.fori_loop(0, tokens, fetch, 0)
-    raw[...] = jnp.zeros_like(raw)
-    nrm[...] = jnp.zeros_like(nrm)
-
-    def take(t, _):
-        entry = local(t)
-
-        @pl.when(owned(t))
+            whole_rows(entry, rank).wait()
+
+        if left:
+            @pl.when(entry >= whole)
+            def _():
+                last_rows(rank).wait()
+
+        return entry % 16
+
+    source = jnp.full((SLOTS, 1), -1, jnp.int32)
+    slot = lax.broadcasted_iota(jnp.int32, (SLOTS, 1), 0)
+    for rank in range(SLOTS):
+        @pl.when(rank < held)
         def _():
-            pltpu.make_async_copy(tail_ref, buf.at[t], sems.at[t]).wait()
-            at = jnp.where(entry < whole, entry % 16, entry - (vocab_rows - 16))
-            picked = lax.broadcasted_iota(jnp.int32, (16, width), 0) == at
-            row = jnp.sum(
-                jnp.where(picked, buf[t].astype(F32), 0.0), axis=0, keepdims=True
+            arrive(rank)
+
+        at = jnp.where(rank < held, rank * 16 + entries[rank] % 16, -1)
+        source = jnp.where(slot == rank, at, source)
+    select = (
+        lax.broadcasted_iota(jnp.int32, (SLOTS, SLOTS * 16), 1) == source
+    ).astype(BF16)
+    rows = jnp.dot(
+        select, buf[0:SLOTS].reshape(SLOTS * 16, width), preferred_element_type=F32
+    )
+    gain_copy.wait()
+    scale = lax.rsqrt(jnp.mean(rows * rows, axis=-1, keepdims=True) + EPS_NORM)
+    first = rows * scale * gain[...]
+    for b in range(dp * tp):
+        rest = jnp.concatenate(
+            [
+                first[:, depth * b + 128 : depth * (b + 1)],
+                jnp.zeros((SLOTS, 256 - depth), F32),
+            ],
+            axis=1,
+        )
+        msg_ref[b] = jnp.concatenate(
+            [first[:, depth * b : depth * b + 128], rest], axis=0
+        ).astype(BF16)
+    raw_ref[0:SLOTS] = rows.astype(BF16)
+
+    @pl.when(held > SLOTS)
+    def _():
+        raw[...] = jnp.zeros_like(raw)
+        raw[0:SLOTS] = rows
+
+        def take(rank, _):
+            picked = lax.broadcasted_iota(jnp.int32, (16, width), 0) == arrive(rank)
+            raw[pl.ds(rank, 1), :] = jnp.sum(
+                jnp.where(picked, buf[rank].astype(F32), 0.0), axis=0, keepdims=True
             )
-            meansq = jnp.mean(row * row, axis=-1, keepdims=True)
-            raw[pl.ds(t, 1), :] = row
-            nrm[pl.ds(t, 1), :] = row * lax.rsqrt(meansq + EPS_NORM) * gain_ref[...]
-
-        return 0
-
-    lax.fori_loop(0, tokens, take, 0)
-    own_ref[...] = raw[...].astype(BF16)
-    quarter = tokens // 4
-
-    def block(b):
-        main = nrm[:, depth * b : depth * b + 128]
-        rest = nrm[:, depth * b + 128 : depth * (b + 1)]
-        rest = jnp.concatenate(
-            [rest[quarter * i : quarter * (i + 1)] for i in range(4)], axis=1
-        )
-        return jnp.concatenate([main, rest], axis=0)
-
-    even = my_dp % 2 == 0
-    for x in range(dp // 2):
-        for t in range(tp):
-            at_even = block((2 * x) * tp + t)
-            at_odd = block((2 * x + 1) * tp + t)
-            keep_ref[x * tp + t] = jnp.where(even, at_even, at_odd).astype(BF16)
-            send_ref[x * tp + t] = jnp.where(even, at_odd, at_even).astype(BF16)
+            return 0
+
+        lax.fori_loop(SLOTS, held, take, 0)
+        raw_ref[...] = raw[...].astype(BF16)
 
 
 def by_core(rows, dp, per_dp):
@@ -122,23 +180,31 @@
     return jnp.concatenate(mine + other, axis=0)
 
 
-def project_kernel(dp, tp, blocks_ref, weight_ref, keep_ref, send_ref):
-    tokens = 64
+def project_kernel(dp, tp, place_ref, msg_ref, extra_ref, weight_ref, keep_ref, send_ref):
+    tokens = place_ref.shape[0]
     per_dp = tokens // dp
-    quarter = tokens // 4
     width = HEADS * HEAD
     kv_width = KV_HEADS * HEAD
-    total = jnp.sum(blocks_ref[...].astype(F32), axis=0)
-    main = by_core(total[:tokens], dp, per_dp).astype(BF16)
-    rest = total[tokens:]
-    rest = jnp.concatenate([rest[:, 32 * i : 32 * (i + 1)] for i in range(4)], axis=0)
-    rest = by_core(rest, dp, per_dp).astype(BF16)
+    slots = dp * tp * SLOTS
+    blocks = msg_ref[...].astype(F32)
+    place = place_ref[:, 0:1]
+    holder, rank = place // tokens, place % tokens
+    place = jnp.where(rank < SLOTS, holder * SLOTS + rank, -1)
+    select = (lax.broadcasted_iota(jnp.int32, (tokens, slots), 1) == place).astype(BF16)
+    extra = extra_ref[...].astype(F32)
+
+    def pick(rows, more):
+        rows = rows.reshape(slots, 128).astype(BF16)
+        return (jnp.dot(select, rows, preferred_element_type=F32) + more).astype(BF16)
+
+    main = pick(blocks[:, :SLOTS], extra[:, :128])
+    rest = pick(blocks[:, SLOTS:], extra[:, 128:])[:, : weight_ref.shape[0] - 128]
     half = tokens // 2
 
     def dot(at, size):
         return jnp.dot(
             main, weight_ref[0:128, at : at + size], preferred_element_type=F32
-        ) + jnp.dot(rest, weight_ref[128:160, at : at + size], preferred_element_type=F32)
+        ) + jnp.dot(rest, weight_ref[128:, at : at + size], preferred_element_type=F32)
 
     for g in range(tp):
         spans = (
@@ -155,87 +221,112 @@
                 ]
 
 
-def attend_kernel(dp, tp, lengths_ref, qkv_ref, keys_ref, values_ref, msg_ref, joined, level):
-    g = pl.program_id(0)
-    rows, span = keys_ref.shape[0], keys_ref.shape[1]
+def attend_kernel(dp, tp, lengths_ref, qkv_ref, keys_ref, values_ref, msg_ref,
+                  keys, values, scores_of, probs_of, weighted_of, joined, key_sems, value_sems):
+    rows, span = keys.shape[0], keys.shape[1]
     per_dp = rows * STEPS
     lines = GROUP * per_dp
     my_tp = lax.axis_index("tp")
     depth = HEADS * HEAD // (dp * tp)
     scale = HEAD ** (-0.5)
-
-    packed = qkv_ref[0]
-    queries = jnp.concatenate(
-        [packed[:, HEAD * h : HEAD * (h + 1)] for h in range(GROUP)], axis=0
-    )
-    fresh_keys = packed[:, GROUP * HEAD : (GROUP + 1) * HEAD]
-    fresh_values = packed[:, (GROUP + 1) * HEAD :]
     nt = (((1,), (1,)), ((), ()))
+
+    def copies(source, target, sems):
+        return [
+            pltpu.make_async_copy(source.at[r], target.at[r], sems.at[r]) for r in range(rows)
+        ]
+
+    key_copies = copies(keys_ref, keys, key_sems)
+    value_copies = copies(values_ref, values, value_sems)
+    for copy in key_copies + value_copies:
+        copy.start()
 
     line = lax.broadcasted_iota(jnp.int32, (lines, 1), 0) % per_dp
     row_of = line // STEPS
     length = jnp.zeros((lines, 1), jnp.int32)
-    scores = jnp.zeros((lines, span), F32)
     for r in range(rows):
         length = jnp.where(row_of == r, lengths_ref[r], length)
-        part = lax.dot_general(queries, keys_ref[r], nt, preferred_element_type=F32)
-        scores = jnp.where(row_of == r, part, scores)
     position = my_tp * span + lax.broadcasted_iota(jnp.int32, (lines, span), 1)
     live = position < length
-    scores = jnp.where(live, scores * scale, MASK_LOW)
-
     column = lax.broadcasted_iota(jnp.int32, (lines, per_dp), 1)
-    fresh = lax.dot_general(queries, fresh_keys, nt, preferred_element_type=F32) * scale
-    seen = (column // STEPS == row_of) & (column <= line) & (my_tp == g)
-    fresh = jnp.where(seen, fresh, MASK_LOW)
-
-    top = jnp.maximum(
-        jnp.max(scores, axis=-1, keepdims=True), jnp.max(fresh, axis=-1, keepdims=True)
-    )
-    probs = jnp.where(live, jnp.exp(scores - top), 0.0)
-    fresh_probs = jnp.where(seen, jnp.exp(fresh - top), 0.0)
-    total = jnp.sum(probs, axis=-1, keepdims=True) + jnp.sum(fresh_probs, axis=-1, keepdims=True)
-    weighted = jnp.dot(fresh_probs.astype(BF16), fresh_values, preferred_element_type=F32)
-    probs = probs.astype(BF16)
+    causal = (column // STEPS == row_of) & (column <= line)
+
+    queries = []
+    for g in range(KV_HEADS):
+        queries.append(
+            jnp.concatenate(
+                [qkv_ref[g, :, HEAD * h : HEAD * (h + 1)] for h in range(GROUP)], axis=0
+            )
+        )
     for r in range(rows):
-        weighted += jnp.dot(
-            jnp.where(row_of == r, probs, jnp.zeros_like(probs)),
-            values_ref[r],
-            preferred_element_type=F32,
-        )
-    some = total > 0.0
-    safe = jnp.where(some, total, 1.0)
-    outcome = weighted / safe
-    logsum = jnp.where(some, top + jnp.log(safe), MASK_LOW)
+        key_copies[r].wait()
+        for g in range(KV_HEADS):
+            part = lax.dot_general(
+                queries[g],
+                keys[r, :, HEAD * g : HEAD * (g + 1)],
+                nt,
+                preferred_element_type=F32,
+            )
+            scores_of[g] = part if r == 0 else jnp.where(row_of == r, part, scores_of[g])
+    kept = []
+    for g in range(KV_HEADS):
+        fresh_keys = qkv_ref[g, :, GROUP * HEAD : (GROUP + 1) * HEAD]
+        fresh_values = qkv_ref[g, :, (GROUP + 1) * HEAD :]
+        scores = jnp.where(live, scores_of[g] * scale, MASK_LOW)
+        fresh = lax.dot_general(queries[g], fresh_keys, nt, preferred_element_type=F32) * scale
+        seen = causal & (my_tp == g)
+        fresh = jnp.where(seen, fresh, MASK_LOW)
+        top = jnp.maximum(
+            jnp.max(scores, axis=-1, keepdims=True), jnp.max(fresh, axis=-1, keepdims=True)
+        )
+        probs = jnp.where(live, jnp.exp(scores - top), 0.0)
+        fresh_probs = jnp.where(seen, jnp.exp(fresh - top), 0.0)
+        total = jnp.sum(probs, axis=-1, keepdims=True)
+        total += jnp.sum(fresh_probs, axis=-1, keepdims=True)
+        probs_of[g] = probs.astype(BF16)
+        weighted_of[g] = jnp.dot(
+            fresh_probs.astype(BF16), fresh_values, preferred_element_type=F32
+        )
+        kept.append((top, total))
+    for r in range(rows):
+        value_copies[r].wait()
+        for g in range(KV_HEADS):
+            probs = probs_of[g]
+            weighted_of[g] += jnp.dot(
+                jnp.where(row_of == r, probs, jnp.zeros_like(probs)),
+                values[r, :, HEAD * g : HEAD * (g + 1)],
+                preferred_element_type=F32,
+            )
+
     lane = lax.broadcasted_iota(jnp.int32, (per_dp, HEAD), 1)
-    levels = level[...]
-    for h in range(GROUP):
-        at = pl.multiple_of((g * GROUP + h) * HEAD, HEAD)
-        joined[:, pl.ds(at, HEAD)] = outcome[per_dp * h : per_dp * (h + 1)]
-        levels = jnp.where(
-            lane == g * GROUP + h, logsum[per_dp * h : per_dp * (h + 1)], levels
-        )
-    level[...] = levels
-
-    @pl.when(g == KV_HEADS - 1)
-    def _():
-        final = level[...]
-        high = final.astype(BF16).astype(F32)
-        middle = (final - high).astype(BF16).astype(F32)
-        low = final - high - middle
-        for b in range(dp * tp):
-            h = depth * b // HEAD
-            pieces = [joined[:, depth * b : depth * (b + 1)]]
-            for head in (h, h + 1):
-                for part in (high, middle, low):
-                    pieces.append(part[:, head : head + 1])
-            pieces.append(jnp.zeros((per_dp, 256 - depth - 6), F32))
-            msg_ref[b] = jnp.concatenate(pieces, axis=1).astype(BF16)
-
-
-def output_kernel(dp, tp, msg_ref, weight_ref, own_ref, keep_ref, send_ref):
+    levels = jnp.zeros((per_dp, HEAD), F32)
+    for g in range(KV_HEADS):
+        top, total = kept[g]
+        some = total > 0.0
+        safe = jnp.where(some, total, 1.0)
+        outcome = weighted_of[g] / safe
+        logsum = jnp.where(some, top + jnp.log(safe), MASK_LOW)
+        for h in range(GROUP):
+            head = g * GROUP + h
+            joined[:, HEAD * head : HEAD * (head + 1)] = outcome[per_dp * h : per_dp * (h + 1)]
+            one = logsum[per_dp * h : per_dp * (h + 1)]
+            high = one.astype(BF16).astype(F32)
+            middle = (one - high).astype(BF16).astype(F32)
+            for i, part in enumerate((high, middle, one - high - middle)):
+                levels = jnp.where(lane == 3 * head + i, part, levels)
+    for b in range(dp * tp):
+        at = depth * b
+        turned = pltpu.roll(levels, (depth - 128 - 3 * (at // HEAD)) % 128, 1)
+        rest = jnp.concatenate(
+            [joined[:, at + 128 : at + depth], jnp.zeros((per_dp, 256 - depth), F32)], axis=1
+        )
+        rest = jnp.where(lane < depth - 128, rest, turned)
+        msg_ref[b] = jnp.concatenate([joined[:, at : at + 128], rest], axis=1).astype(BF16)
+
+
+def output_kernel(dp, tp, place_ref, msg_ref, weight_ref, raw_ref, keep_ref, send_ref):
     depth = weight_ref.shape[0]
-    per_dp = msg_ref.shape[1]
+    tokens, per_dp = place_ref.shape[0], msg_ref.shape[1]
     my_block = lax.axis_index("dp") * tp + lax.axis_index("tp")
     edge = HEAD - (depth * my_block) % HEAD
     first_head = lax.broadcasted_iota(jnp.int32, (per_dp, depth), 1) < edge
@@ -258,15 +349,22 @@
             weighted += share * part
         merged.append(weighted / total)
     attended = by_core(jnp.concatenate(merged, axis=0), dp, per_dp).astype(BF16)
-    half = dp // 2 * per_dp
+    place = place_ref[:, 0:1] - my_block * tokens
+    select = (lax.broadcasted_iota(jnp.int32, (tokens, tokens), 1) == place).astype(BF16)
+    half = tokens // 2
     out_width = weight_ref.shape[1] // tp
     for t in range(tp):
         cols = slice(out_width * t, out_width * (t + 1))
         part = jnp.dot(attended, weight_ref[:, cols], preferred_element_type=F32)
-        part += by_core(own_ref[:, cols].astype(F32), dp, per_dp)
+        part += jnp.dot(select, raw_ref[:, cols], preferred_element_type=F32)
         for x in range(dp // 2):
             keep_ref[x * tp + t] = part[per_dp * x : per_dp * (x + 1)]
             send_ref[x * tp + t] = part[half + per_dp * x : half + per_dp * (x + 1)]
+
+
+def finish_kernel(sums_ref, out_ref):
+    total = jnp.sum(sums_ref[...].astype(F32), axis=0)
+    out_ref[...] = total.reshape(out_ref.shape).astype(BF16)
 
 
 def whole(shape_count):
@@ -297,10 +395,12 @@
     tokens = per_dp * dp
     half = dp // 2 * tp
     depth = width // (dp * tp)
-    packed = width // (dp * tp) * tokens // 128
     out_width = width // tp
     joined_width = (GROUP + 2) * HEAD
-    params = pltpu.CompilerParams(vmem_limit_bytes=VMEM_LIMIT)
+
+    def granted(size):
+        return pltpu.CompilerParams(vmem_limit_bytes=size * MIB)
+
 
     core_pairs = [
         (d * tp + t, (d ^ 1) * tp + t) for d in range(dp) for t in range(tp)
@@ -315,30 +415,54 @@
     def among_chips(value):
         return lax.all_to_all(value, BOTH, 0, 0, tiled=True, axis_index_groups=same_core)
 
-    keep, send, own_rows = pl.pallas_call(
+    message, raw_rows, place, most = pl.pallas_call(
         functools.partial(lookup_kernel, dp, tp),
         out_shape=(
-            jax.ShapeDtypeStruct((half, packed, 128), BF16),
-            jax.ShapeDtypeStruct((half, packed, 128), BF16),
+            jax.ShapeDtypeStruct((dp * tp, 2 * SLOTS, 128), BF16),
             jax.ShapeDtypeStruct((tokens, width), BF16),
+            jax.ShapeDtypeStruct((tokens, 128), jnp.int32),
+            jax.ShapeDtypeStruct((1,), jnp.int32),
         ),
         in_specs=[
             pl.BlockSpec(memory_space=pltpu.SMEM),
             pl.BlockSpec(memory_space=pl.ANY),
             pl.BlockSpec(memory_space=pl.ANY),
-            pl.BlockSpec(memory_space=pltpu.VMEM),
         ],
-        out_specs=tuple(whole(3)),
+        out_specs=tuple(whole(3)) + (pl.BlockSpec(memory_space=pltpu.SMEM),),
         scratch_shapes=[
             pltpu.VMEM((tokens, 16, width), BF16),
+            pltpu.VMEM((1, width), F32),
             pltpu.VMEM((tokens, width), F32),
-            pltpu.VMEM((tokens, width), F32),
+            pltpu.VMEM((tokens, 128), jnp.int32),
+            pltpu.SMEM((tokens + 1,), jnp.int32),
             pltpu.SemaphoreType.DMA((tokens,)),
+            pltpu.SemaphoreType.DMA,
         ],
-        compiler_params=params,
+        compiler_params=granted(48),
         name="lookup",
-    )(token_ids, embed_table, embed_table[-16:], norm_gain.reshape(1, width))
-    blocks = among_chips(keep + other_core(send))
+    )(token_ids.T, embed_table, norm_gain.reshape(1, width))
+
+    arrived = lax.all_to_all(message, BOTH, 0, 0, tiled=True)
+
+    def one_more(state):
+        k, found = state
+        rows = lax.dynamic_slice_in_dim(raw_rows, k * SLOTS, SLOTS, 0).astype(F32)
+        meansq = jnp.mean(rows * rows, axis=-1, keepdims=True)
+        rows = (rows * lax.rsqrt(meansq + EPS_NORM) * norm_gain).astype(BF16)
+        rows = rows.reshape(SLOTS, dp * tp, depth).transpose(1, 0, 2)
+        rows = lax.all_to_all(rows, BOTH, 0, 0, tiled=True).reshape(-1, depth)
+        holder, rank = place[:, :1] // tokens, place[:, :1] % tokens
+        at = jnp.where(rank // SLOTS == k, holder * SLOTS + rank % SLOTS, -1)
+        select = (at == jnp.arange(dp * tp * SLOTS, dtype=jnp.int32)).astype(BF16)
+        rows = jnp.dot(select, rows, preferred_element_type=F32).astype(BF16)
+        return k + 1, found + jnp.pad(rows, ((0, 0), (0, 256 - depth)))
+
+    def all_more(rounds):
+        return lax.while_loop(
+            lambda state: state[0] <= rounds,
+            one_more,
+            (jnp.int32(1), jnp.zeros((tokens, 256), BF16)),
+        )[1]
 
     qkv_master_new, qkv_first_new, qkv_second_new = adamw(
         qkv_master, qkv_first, qkv_second, qkv_grad
@@ -348,15 +472,17 @@
     )
     qkv_half = qkv_master_new.astype(BF16)
     out_half = out_master_new.astype(BF16)
+    arrived, most = lax.optimization_barrier((arrived, most))
+    extra = all_more(most[0] // SLOTS)
 
     keep, send = pl.pallas_call(
         functools.partial(project_kernel, dp, tp),
         out_shape=(jax.ShapeDtypeStruct((half, per_dp, joined_width), F32),) * 2,
-        in_specs=whole(2),
+        in_specs=whole(4),
         out_specs=tuple(whole(2)),
-        compiler_params=params,
+        compiler_params=granted(16),
         name="project",
-    )(blocks, qkv_half)
+    )(place, arrived, extra, qkv_half)
     partial = among_chips(keep + other_core(send))
     projected = jnp.sum(partial, axis=0).astype(BF16)
     joined = lax.all_to_all(
@@ -365,17 +491,25 @@
 
     messages = pl.pallas_call(
         functools.partial(attend_kernel, dp, tp),
-        grid=(KV_HEADS,),
         out_shape=jax.ShapeDtypeStruct((dp * tp, per_dp, 256), BF16),
         in_specs=[
             pl.BlockSpec(memory_space=pltpu.SMEM),
-            pl.BlockSpec((1, per_dp, joined_width), lambda g: (g, 0, 0)),
-            pl.BlockSpec((group_rows, span, HEAD), lambda g: (0, 0, g)),
-            pl.BlockSpec((group_rows, span, HEAD), lambda g: (0, 0, g)),
+            pl.BlockSpec(memory_space=pltpu.VMEM),
+            pl.BlockSpec(memory_space=pltpu.HBM),
+            pl.BlockSpec(memory_space=pltpu.HBM),
         ],
-        out_specs=pl.BlockSpec((dp * tp, per_dp, 256), lambda g: (0, 0, 0)),
-        scratch_shapes=[pltpu.VMEM((per_dp, width), F32), pltpu.VMEM((per_dp, HEAD), F32)],
-        compiler_params=params,
+        out_specs=pl.BlockSpec(memory_space=pltpu.VMEM),
+        scratch_shapes=[
+            pltpu.VMEM((group_rows, span, cache_keys.shape[2]), BF16),
+            pltpu.VMEM((group_rows, span, cache_keys.shape[2]), BF16),
+            pltpu.VMEM((KV_HEADS, GROUP * per_dp, span), F32),
+            pltpu.VMEM((KV_HEADS, GROUP * per_dp, span), BF16),
+            pltpu.VMEM((KV_HEADS, GROUP * per_dp, HEAD), F32),
+            pltpu.VMEM((per_dp, width), F32),
+            pltpu.SemaphoreType.DMA((group_rows,)),
+            pltpu.SemaphoreType.DMA((group_rows,)),
+        ],
+        compiler_params=granted(56),
         name="attend",
     )(cache_lengths, joined, cache_keys, cache_values)
     arrived = lax.all_to_all(messages, BOTH, 0, 0, tiled=True)
@@ -383,13 +517,20 @@
     keep, send = pl.pallas_call(
         functools.partial(output_kernel, dp, tp),
         out_shape=(jax.ShapeDtypeStruct((half, per_dp, out_width), F32),) * 2,
-        in_specs=whole(3),
+        in_specs=whole(4),
         out_specs=tuple(whole(2)),
-        compiler_params=params,
+        compiler_params=granted(16),
         name="output",
-    )(arrived, out_half, own_rows)
+    )(place, arrived, out_half, raw_rows)
     sums = among_chips((keep + other_core(send)).astype(BF16))
-    layer_out = jnp.sum(sums.astype(F32), axis=0).astype(BF16)
+    layer_out = pl.pallas_call(
+        finish_kernel,
+        out_shape=jax.ShapeDtypeStruct((group_rows, STEPS, out_width), BF16),
+        in_specs=whole(1),
+        out_specs=whole(1)[0],
+        compiler_params=granted(16),
+        name="finish",
+    )(sums)
     return (
         qkv_master_new,
         qkv_first_new,
@@ -397,7 +538,7 @@
         out_master_new,
         out_first_new,
         out_second_new,
-        layer_out.reshape(group_rows, STEPS, out_width),
+        layer_out,
     )
 
 

time: 122 us -> 115 us (0.943)
  local copies, waits for them, and re-layouts: 5.26 us -> 0.93 us
  between operations: 0.72 us -> 3.38 us
  waiting for transfers between devices: 9.26 us -> 6.8 us
  Pallas kernels: 17.8 us -> 16.1 us
    unnamed x7 -> x4, local copies, waits for them, and re-layouts: 3.68 us -> 0.68 us
    ppermute x3 -> x2, waiting for transfers between devices: 5.91 us -> 4.3 us  [other_core(): return lax.ppermute(value, BOTH, core_pairs)]
    pallas_call x1, Pallas kernels: 6.91 us -> 5.54 us  [on_device_partial(): pl.pallas_call(functools.partial(lookup_kernel, dp, tp), out_shape=(jax.S...]
    pallas_call x1 -> x2, Pallas kernels: 9.26 us -> 8.66 us  [the longest x1 7.98 us: on_device_partial(): pl.pallas_call(functools.partial(attend_kernel, dp, tp), out_shape=jax.Sh...]
  transfers between devices with their start and end apart: 5 -> 4, of which waited for: 5 -> 3; matrix products, arithmetic and copies ran while one was open for 16% -> 17% of each run, Pallas kernels for 0% -> 0%
where the time goes in v2:
time: 115 us; the launch traced here: 114 us
  blocking collectives  57.6 us (50%)
  other arithmetic  19.1 us (17%)
  Pallas kernels  16.1 us (14%)
  starting transfers between devices  10.5 us (9%)
  waiting for transfers between devices  6.8 us (6%)
  between operations  3.38 us (3%)
    all_to_all x2, blocking collectives, among_chips(): lax.all_to_all(value, BOTH, 0, 0, tiled=True, axis_index_groups=same_core)  46.4 us
    all_to_all x1, blocking collectives, on_device_partial(): lax.all_to_all(jnp.broadcast_to(projected[None], (tp,) + projected.shape)...  11.2 us
    convert_element_type x1, other arithmetic, on_device_partial(): qkv_half = qkv_master_new.astype(BF16)  10.9 us
    pallas_call x1, Pallas kernels, on_device_partial(): pl.pallas_call(functools.partial(attend_kernel, dp, tp), out_shape=jax.Sh...  7.98 us
    convert_element_type x1, other arithmetic, on_device_partial(): out_half = out_master_new.astype(BF16)  7.97 us
    all_to_all x1, starting transfers between devices, on_device_partial(): arrived = lax.all_to_all(message, BOTH, 0, 0, tiled=True)  7.3 us
    pallas_call x1, Pallas kernels, on_device_partial(): pl.pallas_call(functools.partial(lookup_kernel, dp, tp), out_shape=(jax.S...  5.54 us
    ppermute x2, waiting for transfers between devices, other_core(): return lax.ppermute(value, BOTH, core_pairs)  4.3 us
  transfers between devices with their start and end apart: 4, of which 3 were waited for; matrix products, arithmetic and copies ran while one was open for 17% of the time, Pallas kernels for 0%

profile of v2, /device:TPU:0, one launch (start us, length us, event | category | flops | bytes accessed | tf_op | source)
XLA Modules:
  0.0 114.5 jit_solution(16130314392891943495)
XLA Ops:
  0.6 0.0 copy-start
  0.6 0.7 copy-done
  1.3 5.5 %lookup.1 = (bf16[32,16,128]{2,1,0:T(8,128)(2,1)}, bf16[64,5120]{1,0:T(8,128)(2,1)S(1)}, s32[64,128]{1,0:T(8,128)S(1)}, s32[1]{0:T(128)}) custom-call(s32[2,32]{1,0:T(2,128)S(1)} %bitcast.17, bf16[2376,5120]{1,0:T(8,128)(2,1)} %table_ref.1, f32[1,5120]{1,0:T(1,128)} %bitcast.18), custom_call_target="tpu_custom_call" | custom-call | tf_op jit(solution)/shard_map/lookup/pallas_call | solution.py:418
  6.9 7.3 %all-to-all-start.1 = ((bf16[32,16,128]{2,1,0:T(8,128)(2,1)}), bf16[32,16,128]{2,1,0:T(8,128)(2,1)S(1)}, u32[]{:S(2)}, u32[]{:S(2)}) async-start(bf16[32,16,128]{2,1,0:T(8,128)(2,1)} %get-tuple-element.212), calls=%async_computation.1 | async-start | bytes 262144 | tf_op jit(solution)/shard_map/all_to_all | solution.py:445
  14.2 0.0 copy-start.1
  14.2 10.9 %fusion.14 = (bf16[160,7168]{1,0:T(8,128)(2,1)S(1)}, f32[160,7168]{1,0:T(8,128)}, f32[160,7168]{1,0:T(8,128)}, f32[160,7168]{1,0:T(8,128)}) fusion(f32[160,7168]{1,0:T(8,128)} %param.16, bf16[160,7168]{1,0:T(8,128)(2,1)} %param.19, f32[160,7168]{1,0:T(8,128)} %param.17, f32[160,7168]{1,0:T(8,128)} %param.18), kind=kLoop, calls=%fused_computation.39 | loop fusion | flops 19496960 | bytes 32112640 | tf_op jit(solution)/shard_map/convert_element_type | solution.py:473
  25.1 0.1 copy.25
  25.2 0.1 copy.26
  25.3 0.1 copy.27
  25.4 0.0 all-to-all-done.1.msg_ref
  28.0 0.0 copy-done.1
  28.0 0.9 project.1
  29.0 0.3 collective-permute-start
  29.3 2.2 %collective-permute-done = f32[16,16,896]{2,1,0:T(8,128)S(1)} collective-permute-done((f32[16,16,896]{2,1,0:T(8,128)S(1)}, f32[16,16,896]{2,1,0:T(8,128)S(1)}, u32[]{:S(2)}, u32[]{:S(2)}) %collective-permute-start) | collective-permute-done | bytes 917536 | tf_op jit(solution)/shard_map/ppermute | solution.py:413
  31.5 0.1 add.135
  31.6 30.8 %all_to_all.37 = f32[16,16,896]{2,1,0:T(8,128)S(1)} all-to-all(f32[16,16,896]{2,1,0:T(8,128)S(1)} %add.135), channel_id=1, replica_groups={{0,1,2,3,4,5,6,7,16,17,18,19,20,21,22,23},{8,9,10,11,12,13,14,15,24,25,..., dimensions={0} | all-to-all | bytes 1835008 | tf_op jit(solution)/shard_map/all_to_all | solution.py:416
  62.4 0.1 reduce_sum.24
  62.5 11.2 %all_to_all.38.qkv_ref = bf16[8,16,896]{2,1,0:T(8,128)(2,1)} all-to-all(bf16[8,16,896]{2,1,0:T(8,128)(2,1)S(1)} %broadcast_in_dim.18), channel_id=1, replica_groups=mesh['dp'=4,'tp'=8] {'tp'}, dimensions={0} | all-to-all | bytes 458752 | tf_op jit(solution)/shard_map/all_to_all | solution.py:488
  73.7 8.0 %attend.1 = bf16[32,16,256]{2,1,0:T(8,128)(2,1)} custom-call(s32[8]{0:T(128)} %lengths_ref.1, bf16[8,16,896]{2,1,0:T(8,128)(2,1)} %all_to_all.38.qkv_ref, bf16[8,256,1024]{2,1,0:T(8,128)(2,1)} %keys_ref.1, bf16[8,256,1024]{2,1,0:T(8,128)(2,1)} %values_ref.1), custom_call_target="tpu_custom_call" | custom-call | tf_op jit(solution)/shard_map/attend/pallas_call | solution.py:492
  81.7 2.8 %all-to-all-start.4 = ((bf16[32,16,256]{2,1,0:T(8,128)(2,1)}), bf16[32,16,256]{2,1,0:T(8,128)(2,1)S(1)}, u32[]{:S(2)}, u32[]{:S(2)}) async-start(bf16[32,16,256]{2,1,0:T(8,128)(2,1)} %attend.1), calls=%async_computation.4 | async-start | bytes 524288 | tf_op jit(solution)/shard_map/all_to_all | solution.py:515
  84.4 8.0 %fusion.11 = (bf16[160,5120]{1,0:T(8,128)(2,1)S(1)}, f32[160,5120]{1,0:T(8,128)}, f32[160,5120]{1,0:T(8,128)}, f32[160,5120]{1,0:T(8,128)}) fusion(f32[160,5120]{1,0:T(8,128)} %param.20, bf16[160,5120]{1,0:T(8,128)(2,1)} %param.23, f32[160,5120]{1,0:T(8,128)} %param.21, f32[160,5120]{1,0:T(8,128)} %param.22), kind=kLoop, calls=%fused_computation.38 | loop fusion | flops 13926400 | bytes 22937600 | tf_op jit(solution)/shard_map/convert_element_type | solution.py:474
  92.4 2.5 %all-to-all-done.4.msg_ref = bf16[32,16,256]{2,1,0:T(8,128)(2,1)S(1)} async-done(((bf16[32,16,256]{2,1,0:T(8,128)(2,1)}), bf16[32,16,256]{2,1,0:T(8,128)(2,1)S(1)}, u32[]{:S(2)}, u32[]{:S(2)}) %all-to-all-start.4) | async-done | bytes 262176 | tf_op jit(solution)/shard_map/all_to_all | solution.py:515
  94.9 1.0 output.1
  95.9 0.1 collective-permute-start.1
  96.0 2.1 %collective-permute-done.1 = f32[16,16,640]{2,1,0:T(8,128)S(1)} collective-permute-done((f32[16,16,640]{2,1,0:T(8,128)S(1)}, f32[16,16,640]{2,1,0:T(8,128)S(1)}, u32[]{:S(2)}, u32[]{:S(2)}) %collective-permute-start.1) | collective-permute-done | bytes 655392 | tf_op jit(solution)/shard_map/ppermute | solution.py:413
  98.1 0.1 add_convert_fusion
  98.2 15.6 %all_to_all.39.sums_ref = bf16[16,16,640]{2,1,0:T(8,128)(2,1)S(1)} all-to-all(bf16[16,16,640]{2,1,0:T(8,128)(2,1)S(1)} %add_convert_fusion), channel_id=1, replica_groups={{0,1,2,3,4,5,6,7,16,17,18,19,20,21,22,23},{8,9,10,11,12,13,14,15,24,25,..., dimensions={0} | all-to-all | bytes 655360 | tf_op jit(solution)/shard_map/all_to_all | solution.py:416
  113.8 0.7 finish.1
  (4 shorter events, 0.0 us)
Async XLA Ops:
  0.6 0.7 copy-start
  6.9 18.5 %all-to-all-start.1 = ((bf16[32,16,128]{2,1,0:T(8,128)(2,1)}), bf16[32,16,128]{2,1,0:T(8,128)(2,1)S(1)}, u32[]{:S(2)}, u32[]{:S(2)}) async-start(bf16[32,16,128]{2,1,0:T(8,128)(2,1)} %get-tuple-element.212), calls=%async_computation.1 | async-start | bytes 262144 | tf_op jit(solution)/shard_map/all_to_all | solution.py:445
  14.2 13.8 %copy-start.1 = (f32[5120]{0:T(1024)S(1)}, f32[5120]{0:T(1024)}, u32[]{:S(2)}) copy-start(f32[5120]{0:T(1024)} %param.24) | copy-start | bytes 61444
  29.0 2.5 %collective-permute-start = (f32[16,16,896]{2,1,0:T(8,128)S(1)}, f32[16,16,896]{2,1,0:T(8,128)S(1)}, u32[]{:S(2)}, u32[]{:S(2)}) collective-permute-start(f32[16,16,896]{2,1,0:T(8,128)S(1)} %get-tuple-element.219), channel_id=1, source_target_pairs={{0,8},{1,9},{2,10},{3,11},{4,12},{5,13},{6,14},{7,15},{8,0},{9,1},... | collective-permute-start | bytes 2752520 | tf_op jit(solution)/shard_map/ppermute | solution.py:413
  81.7 13.3 %all-to-all-start.4 = ((bf16[32,16,256]{2,1,0:T(8,128)(2,1)}), bf16[32,16,256]{2,1,0:T(8,128)(2,1)S(1)}, u32[]{:S(2)}, u32[]{:S(2)}) async-start(bf16[32,16,256]{2,1,0:T(8,128)(2,1)} %attend.1), calls=%async_computation.4 | async-start | bytes 524288 | tf_op jit(solution)/shard_map/all_to_all | solution.py:515
  95.9 2.2 %collective-permute-start.1 = (f32[16,16,640]{2,1,0:T(8,128)S(1)}, f32[16,16,640]{2,1,0:T(8,128)S(1)}, u32[]{:S(2)}, u32[]{:S(2)}) collective-permute-start(f32[16,16,640]{2,1,0:T(8,128)S(1)} %get-tuple-element.221), channel_id=1, source_target_pairs={{0,8},{1,9},{2,10},{3,11},{4,12},{5,13},{6,14},{7,15},{8,0},{9,1},... | collective-permute-start | bytes 1966088 | tf_op jit(solution)/shard_map/ppermute | solution.py:413

commit v3 on v2

--- a/solution.py
+++ b/solution.py
@@ -63,35 +63,37 @@
             table_ref.at[pl.ds(whole, left)], buf.at[rank, pl.ds(0, left)], sems.at[rank]
         )
 
-    def fetch(t, held):
-        entry = ids_ref[t % STEPS, t // STEPS] - base
-        mine = jnp.logical_and(entry >= 0, entry < vocab_rows)
-        entries[held] = entry
-
-        @pl.when(jnp.logical_and(mine, entry < whole))
-        def _():
-            whole_rows(entry, held).start()
-
-        if left:
-            @pl.when(jnp.logical_and(mine, entry >= whole))
-            def _():
-                last_rows(held).start()
-
-        return held + mine.astype(jnp.int32)
-
-    buf[0:SLOTS] = jnp.zeros((SLOTS, 16, width), BF16)
-    held = lax.fori_loop(0, tokens, fetch, 0)
-    raw_ref[SLOTS:] = jnp.zeros((tokens - SLOTS, width), BF16)
-
-    def write(t, _):
+    def look(t, held):
+        identity = ids_ref[t % STEPS, t // STEPS]
         group = t // per_dp
         line = (group % 2 ^ my_core) * (tokens // 2) + group // 2 * per_dp + t % per_dp
-        column[pl.ds(line, 1), :] = jnp.full(
-            (1, 128), ids_ref[t % STEPS, t // STEPS], jnp.int32
-        )
+        column[pl.ds(line, 1), :] = jnp.full((1, 128), identity, jnp.int32)
+        entry = identity - base
+        entries[held] = entry
+        mine = jnp.logical_and(entry >= 0, entry < vocab_rows)
+        return held + mine.astype(jnp.int32)
+
+    held = jnp.int32(0)
+    for t in range(tokens):
+        held = look(t, held)
+
+    def fetch(rank, _):
+        entry = entries[rank]
+
+        @pl.when(entry < whole)
+        def _():
+            whole_rows(entry, rank).start()
+
+        if left:
+            @pl.when(entry >= whole)
+            def _():
+                last_rows(rank).start()
+
         return 0
 
-    lax.fori_loop(0, tokens, write, 0, unroll=8)
+    buf[0:SLOTS] = jnp.zeros((SLOTS, 16, width), BF16)
+    lax.fori_loop(0, held, fetch, 0)
+    raw_ref[SLOTS:] = jnp.zeros((tokens - SLOTS, width), BF16)
     line = lax.broadcasted_iota(jnp.int32, (tokens, 128), 0)
     inside = line % (tokens // 2)
     order = (inside // per_dp * 2 + (line // (tokens // 2) ^ my_core)) * per_dp + line % per_dp
@@ -438,7 +440,7 @@
             pltpu.SemaphoreType.DMA((tokens,)),
             pltpu.SemaphoreType.DMA,
         ],
-        compiler_params=granted(48),
+        compiler_params=granted(62),
         name="lookup",
     )(token_ids.T, embed_table, norm_gain.reshape(1, width))
 

time: 115 us -> 112 us (0.974)
  Pallas kernels: 16.1 us -> 14.5 us
    pallas_call x1, Pallas kernels: 5.54 us -> 3.91 us  [on_device_partial(): pl.pallas_call(functools.partial(lookup_kernel, dp, tp), out_shape=(jax.S...]
where the time goes in v3:
time: 112 us
  blocking collectives  57.6 us (51%)
  other arithmetic  19.1 us (17%)
  Pallas kernels  14.5 us (13%)
  starting transfers between devices  10.1 us (9%)
  waiting for transfers between devices  6.98 us (6%)
  between operations  3.38 us (3%)
    all_to_all x2, blocking collectives, among_chips(): lax.all_to_all(value, BOTH, 0, 0, tiled=True, axis_index_groups=same_core)  46.4 us
    all_to_all x1, blocking collectives, on_device_partial(): lax.all_to_all(jnp.broadcast_to(projected[None], (tp,) + projected.shape)...  11.2 us
    convert_element_type x1, other arithmetic, on_device_partial(): qkv_half = qkv_master_new.astype(BF16)  10.9 us
    pallas_call x1, Pallas kernels, on_device_partial(): pl.pallas_call(functools.partial(attend_kernel, dp, tp), out_shape=jax.Sh...  7.98 us
    convert_element_type x1, other arithmetic, on_device_partial(): out_half = out_master_new.astype(BF16)  7.97 us
    all_to_all x1, starting transfers between devices, on_device_partial(): arrived = lax.all_to_all(message, BOTH, 0, 0, tiled=True)  7.15 us
    ppermute x2, waiting for transfers between devices, other_core(): return lax.ppermute(value, BOTH, core_pairs)  4.31 us
    pallas_call x1, Pallas kernels, on_device_partial(): pl.pallas_call(functools.partial(lookup_kernel, dp, tp), out_shape=(jax.S...  3.91 us
  transfers between devices with their start and end apart: 4, of which 3 were waited for; matrix products, arithmetic and copies ran while one was open for 17% of the time, Pallas kernels for 0%

profile of v3, /device:TPU:0, one launch (start us, length us, event | category | flops | bytes accessed | tf_op | source)
XLA Modules:
  0.0 112.0 jit_solution(5729358265440983849)
XLA Ops:
  0.6 3.9 %lookup.1 = (bf16[32,16,128]{2,1,0:T(8,128)(2,1)}, bf16[64,5120]{1,0:T(8,128)(2,1)S(1)}, s32[64,128]{1,0:T(8,128)}, s32[1]{0:T(128)}) custom-call(s32[2,32]{1,0:T(2,128)} %bitcast.18, bf16[2376,5120]{1,0:T(8,128)(2,1)} %table_ref.1, f32[1,5120]{1,0:T(1,128)} %bitcast.17), custom_call_target="tpu_custom_call" | custom-call | tf_op jit(solution)/shard_map/lookup/pallas_call | solution.py:420
  4.6 7.2 %all-to-all-start.1 = ((bf16[32,16,128]{2,1,0:T(8,128)(2,1)}), bf16[32,16,128]{2,1,0:T(8,128)(2,1)S(1)}, u32[]{:S(2)}, u32[]{:S(2)}) async-start(bf16[32,16,128]{2,1,0:T(8,128)(2,1)} %get-tuple-element.212), calls=%async_computation.1 | async-start | bytes 262144 | tf_op jit(solution)/shard_map/all_to_all | solution.py:447
  11.7 0.0 copy-start
  11.7 0.0 copy-start.1
  11.7 10.9 %fusion.14 = (bf16[160,7168]{1,0:T(8,128)(2,1)S(1)}, f32[160,7168]{1,0:T(8,128)}, f32[160,7168]{1,0:T(8,128)}, f32[160,7168]{1,0:T(8,128)}) fusion(f32[160,7168]{1,0:T(8,128)} %param.16, bf16[160,7168]{1,0:T(8,128)(2,1)} %param.19, f32[160,7168]{1,0:T(8,128)} %param.17, f32[160,7168]{1,0:T(8,128)} %param.18), kind=kLoop, calls=%fused_computation.39 | loop fusion | flops 19496960 | bytes 32112640 | tf_op jit(solution)/shard_map/convert_element_type | solution.py:475
  22.7 0.0 copy-done
  22.7 0.1 copy.25
  22.8 0.1 copy.26
  22.9 0.1 copy.27
  22.9 0.0 all-to-all-done.1.msg_ref
  25.6 0.0 copy-done.1
  25.6 1.0 project.1
  26.6 0.3 collective-permute-start
  26.9 2.2 %collective-permute-done = f32[16,16,896]{2,1,0:T(8,128)S(1)} collective-permute-done((f32[16,16,896]{2,1,0:T(8,128)S(1)}, f32[16,16,896]{2,1,0:T(8,128)S(1)}, u32[]{:S(2)}, u32[]{:S(2)}) %collective-permute-start) | collective-permute-done | bytes 917536 | tf_op jit(solution)/shard_map/ppermute | solution.py:415
  29.1 0.1 add.135
  29.2 30.8 %all_to_all.37 = f32[16,16,896]{2,1,0:T(8,128)S(1)} all-to-all(f32[16,16,896]{2,1,0:T(8,128)S(1)} %add.135), channel_id=1, replica_groups={{0,1,2,3,4,5,6,7,16,17,18,19,20,21,22,23},{8,9,10,11,12,13,14,15,24,25,..., dimensions={0} | all-to-all | bytes 1835008 | tf_op jit(solution)/shard_map/all_to_all | solution.py:418
  60.0 0.1 reduce_sum.24
  60.1 11.2 %all_to_all.38.qkv_ref = bf16[8,16,896]{2,1,0:T(8,128)(2,1)} all-to-all(bf16[8,16,896]{2,1,0:T(8,128)(2,1)S(1)} %broadcast_in_dim.18), channel_id=1, replica_groups=mesh['dp'=4,'tp'=8] {'tp'}, dimensions={0} | all-to-all | bytes 458752 | tf_op jit(solution)/shard_map/all_to_all | solution.py:490
  71.2 8.0 %attend.1 = bf16[32,16,256]{2,1,0:T(8,128)(2,1)} custom-call(s32[8]{0:T(128)} %lengths_ref.1, bf16[8,16,896]{2,1,0:T(8,128)(2,1)} %all_to_all.38.qkv_ref, bf16[8,256,1024]{2,1,0:T(8,128)(2,1)} %keys_ref.1, bf16[8,256,1024]{2,1,0:T(8,128)(2,1)} %values_ref.1), custom_call_target="tpu_custom_call" | custom-call | tf_op jit(solution)/shard_map/attend/pallas_call | solution.py:494
  79.2 2.6 %all-to-all-start.4 = ((bf16[32,16,256]{2,1,0:T(8,128)(2,1)}), bf16[32,16,256]{2,1,0:T(8,128)(2,1)S(1)}, u32[]{:S(2)}, u32[]{:S(2)}) async-start(bf16[32,16,256]{2,1,0:T(8,128)(2,1)} %attend.1), calls=%async_computation.4 | async-start | bytes 524288 | tf_op jit(solution)/shard_map/all_to_all | solution.py:517
  81.8 8.0 %fusion.11 = (bf16[160,5120]{1,0:T(8,128)(2,1)S(1)}, f32[160,5120]{1,0:T(8,128)}, f32[160,5120]{1,0:T(8,128)}, f32[160,5120]{1,0:T(8,128)}) fusion(f32[160,5120]{1,0:T(8,128)} %param.20, bf16[160,5120]{1,0:T(8,128)(2,1)} %param.23, f32[160,5120]{1,0:T(8,128)} %param.21, f32[160,5120]{1,0:T(8,128)} %param.22), kind=kLoop, calls=%fused_computation.38 | loop fusion | flops 13926400 | bytes 22937600 | tf_op jit(solution)/shard_map/convert_element_type | solution.py:476
  89.8 2.7 %all-to-all-done.4.msg_ref = bf16[32,16,256]{2,1,0:T(8,128)(2,1)S(1)} async-done(((bf16[32,16,256]{2,1,0:T(8,128)(2,1)}), bf16[32,16,256]{2,1,0:T(8,128)(2,1)S(1)}, u32[]{:S(2)}, u32[]{:S(2)}) %all-to-all-start.4) | async-done | bytes 262176 | tf_op jit(solution)/shard_map/all_to_all | solution.py:517
  92.5 1.0 output.1
  93.5 0.1 collective-permute-start.1
  93.6 2.1 %collective-permute-done.1 = f32[16,16,640]{2,1,0:T(8,128)S(1)} collective-permute-done((f32[16,16,640]{2,1,0:T(8,128)S(1)}, f32[16,16,640]{2,1,0:T(8,128)S(1)}, u32[]{:S(2)}, u32[]{:S(2)}) %collective-permute-start.1) | collective-permute-done | bytes 655392 | tf_op jit(solution)/shard_map/ppermute | solution.py:415
  95.6 0.1 add_convert_fusion
  95.7 15.6 %all_to_all.39.sums_ref = bf16[16,16,640]{2,1,0:T(8,128)(2,1)S(1)} all-to-all(bf16[16,16,640]{2,1,0:T(8,128)(2,1)S(1)} %add_convert_fusion), channel_id=1, replica_groups={{0,1,2,3,4,5,6,7,16,17,18,19,20,21,22,23},{8,9,10,11,12,13,14,15,24,25,..., dimensions={0} | all-to-all | bytes 655360 | tf_op jit(solution)/shard_map/all_to_all | solution.py:418
  111.3 0.7 finish.1
  (4 shorter events, 0.0 us)
Async XLA Ops:
  4.6 18.4 %all-to-all-start.1 = ((bf16[32,16,128]{2,1,0:T(8,128)(2,1)}), bf16[32,16,128]{2,1,0:T(8,128)(2,1)S(1)}, u32[]{:S(2)}, u32[]{:S(2)}) async-start(bf16[32,16,128]{2,1,0:T(8,128)(2,1)} %get-tuple-element.212), calls=%async_computation.1 | async-start | bytes 262144 | tf_op jit(solution)/shard_map/all_to_all | solution.py:447
  11.7 11.0 %copy-start = (s32[64,128]{1,0:T(8,128)S(1)}, s32[64,128]{1,0:T(8,128)}, u32[]{:S(2)}) copy-start(s32[64,128]{1,0:T(8,128)} %get-tuple-element.233.place_ref) | copy-start | bytes 98308
  11.7 13.8 %copy-start.1 = (f32[5120]{0:T(1024)S(1)}, f32[5120]{0:T(1024)}, u32[]{:S(2)}) copy-start(f32[5120]{0:T(1024)} %param.24) | copy-start | bytes 61444
  26.6 2.5 %collective-permute-start = (f32[16,16,896]{2,1,0:T(8,128)S(1)}, f32[16,16,896]{2,1,0:T(8,128)S(1)}, u32[]{:S(2)}, u32[]{:S(2)}) collective-permute-start(f32[16,16,896]{2,1,0:T(8,128)S(1)} %get-tuple-element.219), channel_id=1, source_target_pairs={{0,8},{1,9},{2,10},{3,11},{4,12},{5,13},{6,14},{7,15},{8,0},{9,1},... | collective-permute-start | bytes 2752520 | tf_op jit(solution)/shard_map/ppermute | solution.py:415
  79.2 13.3 %all-to-all-start.4 = ((bf16[32,16,256]{2,1,0:T(8,128)(2,1)}), bf16[32,16,256]{2,1,0:T(8,128)(2,1)S(1)}, u32[]{:S(2)}, u32[]{:S(2)}) async-start(bf16[32,16,256]{2,1,0:T(8,128)(2,1)} %attend.1), calls=%async_computation.4 | async-start | bytes 524288 | tf_op jit(solution)/shard_map/all_to_all | solution.py:517
  93.5 2.2 %collective-permute-start.1 = (f32[16,16,640]{2,1,0:T(8,128)S(1)}, f32[16,16,640]{2,1,0:T(8,128)S(1)}, u32[]{:S(2)}, u32[]{:S(2)}) collective-permute-start(f32[16,16,640]{2,1,0:T(8,128)S(1)} %get-tuple-element.221), channel_id=1, source_target_pairs={{0,8},{1,9},{2,10},{3,11},{4,12},{5,13},{6,14},{7,15},{8,0},{9,1},... | collective-permute-start | bytes 1966088 | tf_op jit(solution)/shard_map/ppermute | solution.py:415

commit v4 on v3

--- a/solution.py
+++ b/solution.py
@@ -208,19 +208,24 @@
             main, weight_ref[0:128, at : at + size], preferred_element_type=F32
         ) + jnp.dot(rest, weight_ref[128:, at : at + size], preferred_element_type=F32)
 
+    my_x, my_tp = lax.axis_index("dp") // 2, lax.axis_index("tp")
+    upper = per_dp // 2
     for g in range(tp):
         spans = (
             (0, g * GROUP * HEAD, GROUP * HEAD),
             (GROUP * HEAD, width + g * HEAD, HEAD),
             ((GROUP + 1) * HEAD, width + kv_width + g * HEAD, HEAD),
         )
+        away = g ^ my_tp
+        in_y, in_z = away % 2, away // 2
         for to, at, size in spans:
             part = dot(at, size)
+            cols = slice(to, to + size)
             for x in range(dp // 2):
-                keep_ref[x * tp + g, :, to : to + size] = part[per_dp * x : per_dp * (x + 1)]
-                send_ref[x * tp + g, :, to : to + size] = part[
-                    half + per_dp * x : half + per_dp * (x + 1)
-                ]
+                in_x = x ^ my_x
+                for ref, start in ((keep_ref, per_dp * x), (send_ref, half + per_dp * x)):
+                    ref[0, in_x, in_y, in_z, :, cols] = part[start : start + upper]
+                    ref[1, in_y, in_x, in_z, :, cols] = part[start + upper : start + per_dp]
 
 
 def attend_kernel(dp, tp, lengths_ref, qkv_ref, keys_ref, values_ref, msg_ref,
@@ -414,6 +419,12 @@
     def other_core(value):
         return lax.ppermute(value, BOTH, core_pairs)
 
+    def neighbour(value, flip):
+        pairs = [
+            (d * tp + t, (d ^ flip[0]) * tp + (t ^ flip[1])) for d in range(dp) for t in range(tp)
+        ]
+        return lax.ppermute(value, BOTH, pairs)
+
     def among_chips(value):
         return lax.all_to_all(value, BOTH, 0, 0, tiled=True, axis_index_groups=same_core)
 
@@ -479,14 +490,32 @@
 
     keep, send = pl.pallas_call(
         functools.partial(project_kernel, dp, tp),
-        out_shape=(jax.ShapeDtypeStruct((half, per_dp, joined_width), F32),) * 2,
+        out_shape=(
+            jax.ShapeDtypeStruct((2, 2, 2, tp // 2, per_dp // 2, joined_width), F32),
+        ) * 2,
         in_specs=whole(4),
         out_specs=tuple(whole(2)),
         compiler_params=granted(16),
         name="project",
     )(place, arrived, extra, qkv_half)
-    partial = among_chips(keep + other_core(send))
-    projected = jnp.sum(partial, axis=0).astype(BF16)
+    arrived = other_core(send)
+
+    def fold(across, where):
+        pairs = [(mine[0], neighbour(mine[1], flip)) for mine, flip in zip(across, where)]
+        return [near + came for near, came in pairs]
+
+    halves = [
+        [keep[i, j] + arrived[i, j] for j in range(2)] for i in range(2)
+    ]
+    halves = fold(halves, ((2, 0), (0, 1)))
+    halves = fold(halves, ((0, 1), (2, 0)))
+    total = jnp.concatenate(halves, axis=1)
+    flip = tp // 2
+    while total.shape[0] > 1:
+        count = total.shape[0] // 2
+        total = total[:count] + neighbour(total[count:], (0, flip))
+        flip //= 2
+    projected = total[0].astype(BF16)
     joined = lax.all_to_all(
         jnp.broadcast_to(projected[None], (tp,) + projected.shape), "tp", 0, 0, tiled=True
     )

time: 112 us -> 110 us (0.982)
  blocking collectives: 57.6 us -> 28.1 us
  waiting for transfers between devices: 6.98 us -> 25.4 us
  starting transfers between devices: 10.1 us -> 18.9 us
    all_to_all x2 -> x1, blocking collectives: 46.4 us -> 15.6 us  [among_chips(): lax.all_to_all(value, BOTH, 0, 0, tiled=True, axis_index_groups=same_core)]
    ppermute x0 -> x6, waiting for transfers between devices: none -> 18.6 us  [neighbour(): return lax.ppermute(value, BOTH, pairs)]
    ppermute x0 -> x6, starting transfers between devices: none -> 8.36 us  [neighbour(): return lax.ppermute(value, BOTH, pairs)]
    all_to_all x1, blocking collectives: 11.2 us -> 12.4 us  [on_device_partial(): lax.all_to_all(jnp.broadcast_to(projected[None], (tp,) + projected.shape)...]
  transfers between devices with their start and end apart: 4 -> 10, of which waited for: 3 -> 9; matrix products, arithmetic and copies ran while one was open for 17% -> 17% of each run, Pallas kernels for 0% -> 0%
where the time goes in v4:
time: 110 us
  blocking collectives  28.1 us (26%)
  waiting for transfers between devices  25.4 us (23%)
  other arithmetic  19.2 us (17%)
  starting transfers between devices  18.9 us (17%)
  Pallas kernels  14.4 us (13%)
  between operations  3.42 us (3%)
    ppermute x6, waiting for transfers between devices, neighbour(): return lax.ppermute(value, BOTH, pairs)  18.6 us
    all_to_all x1, blocking collectives, among_chips(): lax.all_to_all(value, BOTH, 0, 0, tiled=True, axis_index_groups=same_core)  15.6 us
    all_to_all x1, blocking collectives, on_device_partial(): lax.all_to_all(jnp.broadcast_to(projected[None], (tp,) + projected.shape)...  12.4 us
    convert_element_type x1, other arithmetic, on_device_partial(): qkv_half = qkv_master_new.astype(BF16)  10.9 us
    ppermute x6, starting transfers between devices, neighbour(): return lax.ppermute(value, BOTH, pairs)  8.36 us
    pallas_call x1, Pallas kernels, on_device_partial(): pl.pallas_call(functools.partial(attend_kernel, dp, tp), out_shape=jax.Sh...  7.97 us
    convert_element_type x1, other arithmetic, on_device_partial(): out_half = out_master_new.astype(BF16)  7.97 us
    all_to_all x1, starting transfers between devices, on_device_partial(): arrived = lax.all_to_all(message, BOTH, 0, 0, tiled=True)  7.38 us
  transfers between devices with their start and end apart: 10, of which 9 were waited for; matrix products, arithmetic and copies ran while one was open for 17% of the time, Pallas kernels for 0%

profile of v4, /device:TPU:0, one launch (start us, length us, event | category | flops | bytes accessed | tf_op | source)
XLA Modules:
  0.0 109.7 jit_solution(17226721873869702027)
XLA Ops:
  0.6 3.8 %lookup.1 = (bf16[32,16,128]{2,1,0:T(8,128)(2,1)}, bf16[64,5120]{1,0:T(8,128)(2,1)S(1)}, s32[64,128]{1,0:T(8,128)}, s32[1]{0:T(128)}) custom-call(s32[2,32]{1,0:T(2,128)} %bitcast.44, bf16[2376,5120]{1,0:T(8,128)(2,1)} %table_ref.1, f32[1,5120]{1,0:T(1,128)} %bitcast.43), custom_call_target="tpu_custom_call" | custom-call | tf_op jit(solution)/shard_map/lookup/pallas_call | solution.py:431
  4.5 7.4 %all-to-all-start.1 = ((bf16[32,16,128]{2,1,0:T(8,128)(2,1)}), bf16[32,16,128]{2,1,0:T(8,128)(2,1)S(1)}, u32[]{:S(2)}, u32[]{:S(2)}) async-start(bf16[32,16,128]{2,1,0:T(8,128)(2,1)} %get-tuple-element.212), calls=%async_computation.1 | async-start | bytes 262144 | tf_op jit(solution)/shard_map/all_to_all | solution.py:458
  11.9 0.0 copy-start
  11.9 0.0 copy-start.1
  11.9 10.9 %fusion.26 = (bf16[160,7168]{1,0:T(8,128)(2,1)S(1)}, f32[160,7168]{1,0:T(8,128)}, f32[160,7168]{1,0:T(8,128)}, f32[160,7168]{1,0:T(8,128)}) fusion(f32[160,7168]{1,0:T(8,128)} %param.16, bf16[160,7168]{1,0:T(8,128)(2,1)} %param.19, f32[160,7168]{1,0:T(8,128)} %param.17, f32[160,7168]{1,0:T(8,128)} %param.18), kind=kLoop, calls=%fused_computation.63 | loop fusion | flops 19496960 | bytes 32112640 | tf_op jit(solution)/shard_map/convert_element_type | solution.py:486
  22.8 0.0 copy-done
  22.8 0.1 copy.25
  22.9 0.1 copy.26
  23.0 0.1 copy.27
  23.1 0.0 all-to-all-done.1.msg_ref
  25.7 0.0 copy-done.1
  25.8 1.0 project.1
  26.7 0.3 collective-permute-start
  27.0 2.2 %collective-permute-done = f32[2,2,2,4,8,896]{5,4,3,2,1,0:T(8,128)S(1)} collective-permute-done((f32[2,2,2,4,8,896]{5,4,3,2,1,0:T(8,128)S(1)}, f32[2,2,2,4,8,896]{5,4,3,2,1,0:T(8,128)S(1)}, u32[]{:S(2)}, u32[]{:S(2)}) %collective-permute-start) | collective-permute-done | bytes 917536 | tf_op jit(solution)/shard_map/ppermute | solution.py:420
  29.3 1.8 %collective-permute-start.1 = (f32[2,4,8,896]{3,2,1,0:T(8,128)S(1)}, f32[2,4,8,896]{3,2,1,0:T(8,128)S(1)}, u32[]{:S(2)}, u32[]{:S(2)}) collective-permute-start(f32[2,4,8,896]{3,2,1,0:T(8,128)S(1)} %get-tuple-element.264), channel_id=1, source_target_pairs={{0,16},{1,17},{2,18},{3,19},{4,20},{5,21},{6,22},{7,23},{8,24},{9,... | collective-permute-start | bytes 688136 | tf_op jit(solution)/shard_map/ppermute | solution.py:426
  31.1 1.5 %collective-permute-start.3 = (f32[2,4,8,896]{3,2,1,0:T(8,128)S(1)}, f32[2,4,8,896]{3,2,1,0:T(8,128)S(1)}, u32[]{:S(2)}, u32[]{:S(2)}) collective-permute-start(f32[2,4,8,896]{3,2,1,0:T(8,128)S(1)} %get-tuple-element.265), channel_id=1, source_target_pairs={{0,1},{1,0},{2,3},{3,2},{4,5},{5,4},{6,7},{7,6},{8,9},{9,8},{10,11... | collective-permute-start | bytes 688136 | tf_op jit(solution)/shard_map/ppermute | solution.py:426
  32.6 4.5 %collective-permute-done.1 = f32[2,4,8,896]{3,2,1,0:T(8,128)S(1)} collective-permute-done((f32[2,4,8,896]{3,2,1,0:T(8,128)S(1)}, f32[2,4,8,896]{3,2,1,0:T(8,128)S(1)}, u32[]{:S(2)}, u32[]{:S(2)}) %collective-permute-start.1) | collective-permute-done | bytes 229408 | tf_op jit(solution)/shard_map/ppermute | solution.py:426
  37.1 1.4 %collective-permute-done.3 = f32[2,4,8,896]{3,2,1,0:T(8,128)S(1)} collective-permute-done((f32[2,4,8,896]{3,2,1,0:T(8,128)S(1)}, f32[2,4,8,896]{3,2,1,0:T(8,128)S(1)}, u32[]{:S(2)}, u32[]{:S(2)}) %collective-permute-start.3) | collective-permute-done | bytes 229408 | tf_op jit(solution)/shard_map/ppermute | solution.py:426
  38.5 0.1 fusion.16
  38.6 1.5 %collective-permute-start.2 = (f32[4,8,896]{2,1,0:T(8,128)S(1)}, f32[4,8,896]{2,1,0:T(8,128)S(1)}, u32[]{:S(2)}, u32[]{:S(2)}) collective-permute-start(f32[4,8,896]{2,1,0:T(8,128)S(1)} %slice_bitcast_fusion.2), channel_id=1, source_target_pairs={{0,1},{1,0},{2,3},{3,2},{4,5},{5,4},{6,7},{7,6},{8,9},{9,8},{10,11... | collective-permute-start | bytes 344072 | tf_op jit(solution)/shard_map/ppermute | solution.py:426
  40.1 0.6 collective-permute-start.4
  40.8 2.7 %collective-permute-done.2 = f32[4,8,896]{2,1,0:T(8,128)S(1)} collective-permute-done((f32[4,8,896]{2,1,0:T(8,128)S(1)}, f32[4,8,896]{2,1,0:T(8,128)S(1)}, u32[]{:S(2)}, u32[]{:S(2)}) %collective-permute-start.2) | collective-permute-done | bytes 114720 | tf_op jit(solution)/shard_map/ppermute | solution.py:426
  43.5 1.5 %collective-permute-done.4 = f32[4,8,896]{2,1,0:T(8,128)S(1)} collective-permute-done((f32[4,8,896]{2,1,0:T(8,128)S(1)}, f32[4,8,896]{2,1,0:T(8,128)S(1)}, u32[]{:S(2)}, u32[]{:S(2)}) %collective-permute-start.4) | collective-permute-done | bytes 114720 | tf_op jit(solution)/shard_map/ppermute | solution.py:426
  45.0 2.5 %collective-permute-start.5 = (f32[2,16,896]{2,1,0:T(8,128)S(1)}, f32[2,16,896]{2,1,0:T(8,128)S(1)}, u32[]{:S(2)}, u32[]{:S(2)}) collective-permute-start(f32[2,16,896]{2,1,0:T(8,128)S(1)} %pad_maximum_fusion), channel_id=1, source_target_pairs={{0,4},{1,5},{2,6},{3,7},{4,0},{5,1},{6,2},{7,3},{8,12},{9,13},{10,... | collective-permute-start | bytes 344072 | tf_op jit(solution)/shard_map/ppermute | solution.py:426
  47.5 4.6 %collective-permute-done.5 = f32[2,16,896]{2,1,0:T(8,128)S(1)} collective-permute-done((f32[2,16,896]{2,1,0:T(8,128)S(1)}, f32[2,16,896]{2,1,0:T(8,128)S(1)}, u32[]{:S(2)}, u32[]{:S(2)}) %collective-permute-start.5) | collective-permute-done | bytes 114720 | tf_op jit(solution)/shard_map/ppermute | solution.py:426
  52.2 0.4 collective-permute-start.6
  52.6 3.8 %collective-permute-done.6 = f32[1,16,896]{2,1,0:T(8,128)S(1)} collective-permute-done((f32[1,16,896]{2,1,0:T(8,128)S(1)}, f32[1,16,896]{2,1,0:T(8,128)S(1)}, u32[]{:S(2)}, u32[]{:S(2)}) %collective-permute-start.6) | collective-permute-done | bytes 57376 | tf_op jit(solution)/shard_map/ppermute | solution.py:426
  56.4 12.4 %all_to_all.32.qkv_ref = bf16[8,16,896]{2,1,0:T(8,128)(2,1)} all-to-all(bf16[8,16,896]{2,1,0:T(8,128)(2,1)S(1)} %broadcast_in_dim.21), channel_id=1, replica_groups=mesh['dp'=4,'tp'=8] {'tp'}, dimensions={0} | all-to-all | bytes 458752 | tf_op jit(solution)/shard_map/all_to_all | solution.py:519
  68.9 8.0 %attend.1 = bf16[32,16,256]{2,1,0:T(8,128)(2,1)} custom-call(s32[8]{0:T(128)} %lengths_ref.1, bf16[8,16,896]{2,1,0:T(8,128)(2,1)} %all_to_all.32.qkv_ref, bf16[8,256,1024]{2,1,0:T(8,128)(2,1)} %keys_ref.1, bf16[8,256,1024]{2,1,0:T(8,128)(2,1)} %values_ref.1), custom_call_target="tpu_custom_call" | custom-call | tf_op jit(solution)/shard_map/attend/pallas_call | solution.py:523
  76.9 2.8 %all-to-all-start.3 = ((bf16[32,16,256]{2,1,0:T(8,128)(2,1)}), bf16[32,16,256]{2,1,0:T(8,128)(2,1)S(1)}, u32[]{:S(2)}, u32[]{:S(2)}) async-start(bf16[32,16,256]{2,1,0:T(8,128)(2,1)} %attend.1), calls=%async_computation.3 | async-start | bytes 524288 | tf_op jit(solution)/shard_map/all_to_all | solution.py:546
  79.7 8.0 %fusion.23 = (bf16[160,5120]{1,0:T(8,128)(2,1)S(1)}, f32[160,5120]{1,0:T(8,128)}, f32[160,5120]{1,0:T(8,128)}, f32[160,5120]{1,0:T(8,128)}) fusion(f32[160,5120]{1,0:T(8,128)} %param.20, bf16[160,5120]{1,0:T(8,128)(2,1)} %param.23, f32[160,5120]{1,0:T(8,128)} %param.21, f32[160,5120]{1,0:T(8,128)} %param.22), kind=kLoop, calls=%fused_computation.62 | loop fusion | flops 13926400 | bytes 22937600 | tf_op jit(solution)/shard_map/convert_element_type | solution.py:487
  87.6 2.5 %all-to-all-done.3.msg_ref = bf16[32,16,256]{2,1,0:T(8,128)(2,1)S(1)} async-done(((bf16[32,16,256]{2,1,0:T(8,128)(2,1)}), bf16[32,16,256]{2,1,0:T(8,128)(2,1)S(1)}, u32[]{:S(2)}, u32[]{:S(2)}) %all-to-all-start.3) | async-done | bytes 262176 | tf_op jit(solution)/shard_map/all_to_all | solution.py:546
  90.1 1.0 output.1
  91.1 0.1 collective-permute-start.7
  91.2 2.1 %collective-permute-done.7 = f32[16,16,640]{2,1,0:T(8,128)S(1)} collective-permute-done((f32[16,16,640]{2,1,0:T(8,128)S(1)}, f32[16,16,640]{2,1,0:T(8,128)S(1)}, u32[]{:S(2)}, u32[]{:S(2)}) %collective-permute-start.7) | collective-permute-done | bytes 655392 | tf_op jit(solution)/shard_map/ppermute | solution.py:420
  93.3 0.1 add_convert_fusion
  93.4 15.6 %all_to_all.33.sums_ref = bf16[16,16,640]{2,1,0:T(8,128)(2,1)S(1)} all-to-all(bf16[16,16,640]{2,1,0:T(8,128)(2,1)S(1)} %add_convert_fusion), channel_id=1, replica_groups={{0,1,2,3,4,5,6,7,16,17,18,19,20,21,22,23},{8,9,10,11,12,13,14,15,24,25,..., dimensions={0} | all-to-all | bytes 655360 | tf_op jit(solution)/shard_map/all_to_all | solution.py:429
  109.0 0.7 finish.1
  (13 shorter events, 0.2 us)
Async XLA Ops:
  4.5 18.6 %all-to-all-start.1 = ((bf16[32,16,128]{2,1,0:T(8,128)(2,1)}), bf16[32,16,128]{2,1,0:T(8,128)(2,1)S(1)}, u32[]{:S(2)}, u32[]{:S(2)}) async-start(bf16[32,16,128]{2,1,0:T(8,128)(2,1)} %get-tuple-element.212), calls=%async_computation.1 | async-start | bytes 262144 | tf_op jit(solution)/shard_map/all_to_all | solution.py:458
  11.9 11.0 %copy-start = (s32[64,128]{1,0:T(8,128)S(1)}, s32[64,128]{1,0:T(8,128)}, u32[]{:S(2)}) copy-start(s32[64,128]{1,0:T(8,128)} %get-tuple-element.233.place_ref) | copy-start | bytes 98308
  11.9 13.8 %copy-start.1 = (f32[5120]{0:T(1024)S(1)}, f32[5120]{0:T(1024)}, u32[]{:S(2)}) copy-start(f32[5120]{0:T(1024)} %param.24) | copy-start | bytes 61444
  26.7 2.5 %collective-permute-start = (f32[2,2,2,4,8,896]{5,4,3,2,1,0:T(8,128)S(1)}, f32[2,2,2,4,8,896]{5,4,3,2,1,0:T(8,128)S(1)}, u32[]{:S(2)}, u32[]{:S(2)}) collective-permute-start(f32[2,2,2,4,8,896]{5,4,3,2,1,0:T(8,128)S(1)} %get-tuple-element.219), channel_id=1, source_target_pairs={{0,8},{1,9},{2,10},{3,11},{4,12},{5,13},{6,14},{7,15},{8,0},{9,1},... | collective-permute-start | bytes 2752520 | tf_op jit(solution)/shard_map/ppermute | solution.py:420
  29.3 7.8 %collective-permute-start.1 = (f32[2,4,8,896]{3,2,1,0:T(8,128)S(1)}, f32[2,4,8,896]{3,2,1,0:T(8,128)S(1)}, u32[]{:S(2)}, u32[]{:S(2)}) collective-permute-start(f32[2,4,8,896]{3,2,1,0:T(8,128)S(1)} %get-tuple-element.264), channel_id=1, source_target_pairs={{0,16},{1,17},{2,18},{3,19},{4,20},{5,21},{6,22},{7,23},{8,24},{9,... | collective-permute-start | bytes 688136 | tf_op jit(solution)/shard_map/ppermute | solution.py:426
  31.1 7.4 %collective-permute-start.3 = (f32[2,4,8,896]{3,2,1,0:T(8,128)S(1)}, f32[2,4,8,896]{3,2,1,0:T(8,128)S(1)}, u32[]{:S(2)}, u32[]{:S(2)}) collective-permute-start(f32[2,4,8,896]{3,2,1,0:T(8,128)S(1)} %get-tuple-element.265), channel_id=1, source_target_pairs={{0,1},{1,0},{2,3},{3,2},{4,5},{5,4},{6,7},{7,6},{8,9},{9,8},{10,11... | collective-permute-start | bytes 688136 | tf_op jit(solution)/shard_map/ppermute | solution.py:426
  38.6 4.9 %collective-permute-start.2 = (f32[4,8,896]{2,1,0:T(8,128)S(1)}, f32[4,8,896]{2,1,0:T(8,128)S(1)}, u32[]{:S(2)}, u32[]{:S(2)}) collective-permute-start(f32[4,8,896]{2,1,0:T(8,128)S(1)} %slice_bitcast_fusion.2), channel_id=1, source_target_pairs={{0,1},{1,0},{2,3},{3,2},{4,5},{5,4},{6,7},{7,6},{8,9},{9,8},{10,11... | collective-permute-start | bytes 344072 | tf_op jit(solution)/shard_map/ppermute | solution.py:426
  40.1 4.9 %collective-permute-start.4 = (f32[4,8,896]{2,1,0:T(8,128)S(1)}, f32[4,8,896]{2,1,0:T(8,128)S(1)}, u32[]{:S(2)}, u32[]{:S(2)}) collective-permute-start(f32[4,8,896]{2,1,0:T(8,128)S(1)} %slice_bitcast_fusion), channel_id=1, source_target_pairs={{0,16},{1,17},{2,18},{3,19},{4,20},{5,21},{6,22},{7,23},{8,24},{9,... | collective-permute-start | bytes 344072 | tf_op jit(solution)/shard_map/ppermute | solution.py:426
  45.0 7.1 %collective-permute-start.5 = (f32[2,16,896]{2,1,0:T(8,128)S(1)}, f32[2,16,896]{2,1,0:T(8,128)S(1)}, u32[]{:S(2)}, u32[]{:S(2)}) collective-permute-start(f32[2,16,896]{2,1,0:T(8,128)S(1)} %pad_maximum_fusion), channel_id=1, source_target_pairs={{0,4},{1,5},{2,6},{3,7},{4,0},{5,1},{6,2},{7,3},{8,12},{9,13},{10,... | collective-permute-start | bytes 344072 | tf_op jit(solution)/shard_map/ppermute | solution.py:426
  52.2 4.2 %collective-permute-start.6 = (f32[1,16,896]{2,1,0:T(8,128)S(1)}, f32[1,16,896]{2,1,0:T(8,128)S(1)}, u32[]{:S(2)}, u32[]{:S(2)}) collective-permute-start(f32[1,16,896]{2,1,0:T(8,128)S(1)} %slice.90), channel_id=1, source_target_pairs={{0,2},{1,3},{2,0},{3,1},{4,6},{5,7},{6,4},{7,5},{8,10},{9,11},{10,... | collective-permute-start | bytes 172040 | tf_op jit(solution)/shard_map/ppermute | solution.py:426
  76.9 13.3 %all-to-all-start.3 = ((bf16[32,16,256]{2,1,0:T(8,128)(2,1)}), bf16[32,16,256]{2,1,0:T(8,128)(2,1)S(1)}, u32[]{:S(2)}, u32[]{:S(2)}) async-start(bf16[32,16,256]{2,1,0:T(8,128)(2,1)} %attend.1), calls=%async_computation.3 | async-start | bytes 524288 | tf_op jit(solution)/shard_map/all_to_all | solution.py:546
  91.1 2.2 %collective-permute-start.7 = (f32[16,16,640]{2,1,0:T(8,128)S(1)}, f32[16,16,640]{2,1,0:T(8,128)S(1)}, u32[]{:S(2)}, u32[]{:S(2)}) collective-permute-start(f32[16,16,640]{2,1,0:T(8,128)S(1)} %get-tuple-element.221), channel_id=1, source_target_pairs={{0,8},{1,9},{2,10},{3,11},{4,12},{5,13},{6,14},{7,15},{8,0},{9,1},... | collective-permute-start | bytes 1966088 | tf_op jit(solution)/shard_map/ppermute | solution.py:420

commit v5 on v4

--- a/solution.py
+++ b/solution.py
@@ -477,13 +477,10 @@
             (jnp.int32(1), jnp.zeros((tokens, 256), BF16)),
         )[1]
 
-    qkv_master_new, qkv_first_new, qkv_second_new = adamw(
-        qkv_master, qkv_first, qkv_second, qkv_grad
-    )
+    qkv_half = adamw(qkv_master, qkv_first, qkv_second, qkv_grad)[0].astype(BF16)
     out_master_new, out_first_new, out_second_new = adamw(
         out_master, out_first, out_second, out_grad
     )
-    qkv_half = qkv_master_new.astype(BF16)
     out_half = out_master_new.astype(BF16)
     arrived, most = lax.optimization_barrier((arrived, most))
     extra = all_more(most[0] // SLOTS)
@@ -553,7 +550,11 @@
         compiler_params=granted(16),
         name="output",
     )(place, arrived, out_half, raw_rows)
-    sums = among_chips((keep + other_core(send)).astype(BF16))
+    paired, *state = lax.optimization_barrier(
+        ((keep + other_core(send)).astype(BF16), qkv_master, qkv_first, qkv_second, qkv_grad)
+    )
+    sums = among_chips(paired)
+    qkv_master_new, qkv_first_new, qkv_second_new = adamw(*state)
     layer_out = pl.pallas_call(
         finish_kernel,
         out_shape=jax.ShapeDtypeStruct((group_rows, STEPS, out_width), BF16),

time: 110 us -> 108 us (0.982)
  blocking collectives: 28.1 us -> 13.7 us
  other arithmetic: 19.2 us -> 27.4 us
  starting transfers between devices: 18.9 us -> 23.6 us
    all_to_all x1 -> x0, blocking collectives: 15.6 us -> none  [among_chips(): lax.all_to_all(value, BOTH, 0, 0, tiled=True, axis_index_groups=same_core)]
    sub x0 -> x1, other arithmetic: none -> 11 us  [adamw(): master_new = master - LEARN_RATE * (update + WEIGHT_DECAY * master)]
    all_to_all x0 -> x1, starting transfers between devices: none -> 4.18 us  [among_chips(): lax.all_to_all(value, BOTH, 0, 0, tiled=True, axis_index_groups=same_core)]
    convert_element_type x2, other arithmetic: 11 us -> 8.3 us  [the longest x1 7.5 us: on_device_partial(): adamw(qkv_master, qkv_first, qkv_second, qkv_grad)[0].astype(BF16)]
    ppermute x6, waiting for transfers between devices: 18.6 us -> 16.9 us  [neighbour(): return lax.ppermute(value, BOTH, pairs)]
    all_to_all x1, blocking collectives: 12.4 us -> 13.7 us  [on_device_partial(): lax.all_to_all(jnp.broadcast_to(projected[None], (tp,) + projected.shape)...]
  transfers between devices with their start and end apart: 10 -> 11, of which waited for: 9 -> 10; matrix products, arithmetic and copies ran while one was open for 17% -> 25% of each run, Pallas kernels for 0% -> 0%
where the time goes in v5:
time: 108 us; the launch traced here: 107 us
  other arithmetic  27.4 us (25%)
  waiting for transfers between devices  24.4 us (23%)
  starting transfers between devices  23.6 us (22%)
  Pallas kernels  14.4 us (13%)
  blocking collectives  13.7 us (13%)
  between operations  3.44 us (3%)
    ppermute x6, waiting for transfers between devices, neighbour(): return lax.ppermute(value, BOTH, pairs)  16.9 us
    all_to_all x1, blocking collectives, on_device_partial(): lax.all_to_all(jnp.broadcast_to(projected[None], (tp,) + projected.shape)...  13.7 us
    sub x1, other arithmetic, adamw(): master_new = master - LEARN_RATE * (update + WEIGHT_DECAY * master)  11 us
    ppermute x6, starting transfers between devices, neighbour(): return lax.ppermute(value, BOTH, pairs)  8.82 us
    pallas_call x1, Pallas kernels, on_device_partial(): pl.pallas_call(functools.partial(attend_kernel, dp, tp), out_shape=jax.Sh...  7.98 us
    convert_element_type x1, other arithmetic, on_device_partial(): out_half = out_master_new.astype(BF16)  7.97 us
    convert_element_type x1, other arithmetic, on_device_partial(): adamw(qkv_master, qkv_first, qkv_second, qkv_grad)[0].astype(BF16)  7.5 us
    all_to_all x1, starting transfers between devices, on_device_partial(): arrived = lax.all_to_all(message, BOTH, 0, 0, tiled=True)  7.3 us
  transfers between devices with their start and end apart: 11, of which 10 were waited for; matrix products, arithmetic and copies ran while one was open for 25% of the time, Pallas kernels for 0%

profile of v5, /device:TPU:0, one launch (start us, length us, event | category | flops | bytes accessed | tf_op | source)
XLA Modules:
  0.0 107.2 jit_solution(8699088612483175536)
XLA Ops:
  0.6 3.8 %lookup.1 = (bf16[32,16,128]{2,1,0:T(8,128)(2,1)}, bf16[64,5120]{1,0:T(8,128)(2,1)S(1)}, s32[64,128]{1,0:T(8,128)}, s32[1]{0:T(128)}) custom-call(s32[2,32]{1,0:T(2,128)} %bitcast.44, bf16[2376,5120]{1,0:T(8,128)(2,1)} %table_ref.1, f32[1,5120]{1,0:T(1,128)} %bitcast.43), custom_call_target="tpu_custom_call" | custom-call | tf_op jit(solution)/shard_map/lookup/pallas_call | solution.py:431
  4.5 7.3 %all-to-all-start.1 = ((bf16[32,16,128]{2,1,0:T(8,128)(2,1)}), bf16[32,16,128]{2,1,0:T(8,128)(2,1)S(1)}, u32[]{:S(2)}, u32[]{:S(2)}) async-start(bf16[32,16,128]{2,1,0:T(8,128)(2,1)} %get-tuple-element.217), calls=%async_computation.1 | async-start | bytes 262144 | tf_op jit(solution)/shard_map/all_to_all | solution.py:458
  11.8 0.0 copy-start
  11.8 0.0 copy-start.1
  11.8 7.5 %fusion.19.weight_ref = bf16[160,7168]{1,0:T(8,128)(2,1)S(1)} fusion(f32[160,7168]{1,0:T(8,128)} %param.16, f32[160,7168]{1,0:T(8,128)} %param.18, bf16[160,7168]{1,0:T(8,128)(2,1)} %param.19, f32[160,7168]{1,0:T(8,128)} %param.17), kind=kLoop, calls=%fused_computation.43 | loop fusion | flops 19496960 | bytes 18350080 | tf_op jit(solution)/shard_map/convert_element_type | solution.py:480
  19.3 0.0 copy-done
  19.3 0.1 copy.25
  19.4 0.1 copy.27
  19.5 0.1 copy.26
  19.6 0.0 all-to-all-done.1.msg_ref
  22.2 0.0 copy-done.1
  22.3 1.0 project.1
  23.2 0.3 collective-permute-start
  23.5 2.2 %collective-permute-done = f32[2,2,2,4,8,896]{5,4,3,2,1,0:T(8,128)S(1)} collective-permute-done((f32[2,2,2,4,8,896]{5,4,3,2,1,0:T(8,128)S(1)}, f32[2,2,2,4,8,896]{5,4,3,2,1,0:T(8,128)S(1)}, u32[]{:S(2)}, u32[]{:S(2)}) %collective-permute-start) | collective-permute-done | bytes 917536 | tf_op jit(solution)/shard_map/ppermute | solution.py:420
  25.8 1.8 %collective-permute-start.1 = (f32[2,4,8,896]{3,2,1,0:T(8,128)S(1)}, f32[2,4,8,896]{3,2,1,0:T(8,128)S(1)}, u32[]{:S(2)}, u32[]{:S(2)}) collective-permute-start(f32[2,4,8,896]{3,2,1,0:T(8,128)S(1)} %get-tuple-element.273), channel_id=1, source_target_pairs={{0,16},{1,17},{2,18},{3,19},{4,20},{5,21},{6,22},{7,23},{8,24},{9,... | collective-permute-start | bytes 688136 | tf_op jit(solution)/shard_map/ppermute | solution.py:426
  27.6 1.5 %collective-permute-start.3 = (f32[2,4,8,896]{3,2,1,0:T(8,128)S(1)}, f32[2,4,8,896]{3,2,1,0:T(8,128)S(1)}, u32[]{:S(2)}, u32[]{:S(2)}) collective-permute-start(f32[2,4,8,896]{3,2,1,0:T(8,128)S(1)} %get-tuple-element.274), channel_id=1, source_target_pairs={{0,1},{1,0},{2,3},{3,2},{4,5},{5,4},{6,7},{7,6},{8,9},{9,8},{10,11... | collective-permute-start | bytes 688136 | tf_op jit(solution)/shard_map/ppermute | solution.py:426
  29.1 4.5 %collective-permute-done.1 = f32[2,4,8,896]{3,2,1,0:T(8,128)S(1)} collective-permute-done((f32[2,4,8,896]{3,2,1,0:T(8,128)S(1)}, f32[2,4,8,896]{3,2,1,0:T(8,128)S(1)}, u32[]{:S(2)}, u32[]{:S(2)}) %collective-permute-start.1) | collective-permute-done | bytes 229408 | tf_op jit(solution)/shard_map/ppermute | solution.py:426
  33.6 1.4 %collective-permute-done.3 = f32[2,4,8,896]{3,2,1,0:T(8,128)S(1)} collective-permute-done((f32[2,4,8,896]{3,2,1,0:T(8,128)S(1)}, f32[2,4,8,896]{3,2,1,0:T(8,128)S(1)}, u32[]{:S(2)}, u32[]{:S(2)}) %collective-permute-start.3) | collective-permute-done | bytes 229408 | tf_op jit(solution)/shard_map/ppermute | solution.py:426
  35.0 0.1 fusion.27
  35.1 0.4 collective-permute-start.4
  35.5 1.7 %collective-permute-start.2 = (f32[4,8,896]{2,1,0:T(8,128)S(1)}, f32[4,8,896]{2,1,0:T(8,128)S(1)}, u32[]{:S(2)}, u32[]{:S(2)}) collective-permute-start(f32[4,8,896]{2,1,0:T(8,128)S(1)} %slice_bitcast_fusion.2), channel_id=1, source_target_pairs={{0,1},{1,0},{2,3},{3,2},{4,5},{5,4},{6,7},{7,6},{8,9},{9,8},{10,11... | collective-permute-start | bytes 344072 | tf_op jit(solution)/shard_map/ppermute | solution.py:426
  37.3 2.7 %collective-permute-done.4 = f32[4,8,896]{2,1,0:T(8,128)S(1)} collective-permute-done((f32[4,8,896]{2,1,0:T(8,128)S(1)}, f32[4,8,896]{2,1,0:T(8,128)S(1)}, u32[]{:S(2)}, u32[]{:S(2)}) %collective-permute-start.4) | collective-permute-done | bytes 114720 | tf_op jit(solution)/shard_map/ppermute | solution.py:426
  40.0 0.4 collective-permute-done.2
  40.4 2.6 %collective-permute-start.5 = (f32[2,16,896]{2,1,0:T(8,128)S(1)}, f32[2,16,896]{2,1,0:T(8,128)S(1)}, u32[]{:S(2)}, u32[]{:S(2)}) collective-permute-start(f32[2,16,896]{2,1,0:T(8,128)S(1)} %pad_maximum_fusion), channel_id=1, source_target_pairs={{0,4},{1,5},{2,6},{3,7},{4,0},{5,1},{6,2},{7,3},{8,12},{9,13},{10,... | collective-permute-start | bytes 344072 | tf_op jit(solution)/shard_map/ppermute | solution.py:426
  43.1 4.3 %collective-permute-done.5 = f32[2,16,896]{2,1,0:T(8,128)S(1)} collective-permute-done((f32[2,16,896]{2,1,0:T(8,128)S(1)}, f32[2,16,896]{2,1,0:T(8,128)S(1)}, u32[]{:S(2)}, u32[]{:S(2)}) %collective-permute-start.5) | collective-permute-done | bytes 114720 | tf_op jit(solution)/shard_map/ppermute | solution.py:426
  47.4 0.7 collective-permute-start.6
  48.2 3.5 %collective-permute-done.6 = f32[1,16,896]{2,1,0:T(8,128)S(1)} collective-permute-done((f32[1,16,896]{2,1,0:T(8,128)S(1)}, f32[1,16,896]{2,1,0:T(8,128)S(1)}, u32[]{:S(2)}, u32[]{:S(2)}) %collective-permute-start.6) | collective-permute-done | bytes 57376 | tf_op jit(solution)/shard_map/ppermute | solution.py:426
  51.7 13.7 %all_to_all.32.qkv_ref = bf16[8,16,896]{2,1,0:T(8,128)(2,1)} all-to-all(bf16[8,16,896]{2,1,0:T(8,128)(2,1)S(1)} %broadcast_in_dim.21), channel_id=1, replica_groups=mesh['dp'=4,'tp'=8] {'tp'}, dimensions={0} | all-to-all | bytes 458752 | tf_op jit(solution)/shard_map/all_to_all | solution.py:516
  65.4 8.0 %attend.1 = bf16[32,16,256]{2,1,0:T(8,128)(2,1)} custom-call(s32[8]{0:T(128)} %lengths_ref.1, bf16[8,16,896]{2,1,0:T(8,128)(2,1)} %all_to_all.32.qkv_ref, bf16[8,256,1024]{2,1,0:T(8,128)(2,1)} %keys_ref.1, bf16[8,256,1024]{2,1,0:T(8,128)(2,1)} %values_ref.1), custom_call_target="tpu_custom_call" | custom-call | tf_op jit(solution)/shard_map/attend/pallas_call | solution.py:520
  73.4 2.9 %all-to-all-start.3 = ((bf16[32,16,256]{2,1,0:T(8,128)(2,1)}), bf16[32,16,256]{2,1,0:T(8,128)(2,1)S(1)}, u32[]{:S(2)}, u32[]{:S(2)}) async-start(bf16[32,16,256]{2,1,0:T(8,128)(2,1)} %attend.1), calls=%async_computation.3 | async-start | bytes 524288 | tf_op jit(solution)/shard_map/all_to_all | solution.py:543
  76.3 8.0 %fusion.36 = (bf16[160,5120]{1,0:T(8,128)(2,1)S(1)}, f32[160,5120]{1,0:T(8,128)}, f32[160,5120]{1,0:T(8,128)}, f32[160,5120]{1,0:T(8,128)}) fusion(f32[160,5120]{1,0:T(8,128)} %param.20, bf16[160,5120]{1,0:T(8,128)(2,1)} %param.23, f32[160,5120]{1,0:T(8,128)} %param.21, f32[160,5120]{1,0:T(8,128)} %param.22), kind=kLoop, calls=%fused_computation.75 | loop fusion | flops 13926400 | bytes 22937600 | tf_op jit(solution)/shard_map/convert_element_type | solution.py:484
  84.3 2.5 %all-to-all-done.3.msg_ref = bf16[32,16,256]{2,1,0:T(8,128)(2,1)S(1)} async-done(((bf16[32,16,256]{2,1,0:T(8,128)(2,1)}), bf16[32,16,256]{2,1,0:T(8,128)(2,1)S(1)}, u32[]{:S(2)}, u32[]{:S(2)}) %all-to-all-start.3) | async-done | bytes 262176 | tf_op jit(solution)/shard_map/all_to_all | solution.py:543
  86.8 1.0 output.1
  87.8 0.1 collective-permute-start.7
  87.9 2.1 %collective-permute-done.7 = f32[16,16,640]{2,1,0:T(8,128)S(1)} collective-permute-done((f32[16,16,640]{2,1,0:T(8,128)S(1)}, f32[16,16,640]{2,1,0:T(8,128)S(1)}, u32[]{:S(2)}, u32[]{:S(2)}) %collective-permute-start.7) | collective-permute-done | bytes 655392 | tf_op jit(solution)/shard_map/ppermute | solution.py:420
  89.9 0.8 add_convert_fusion
  90.7 4.2 %all-to-all-start.4 = ((bf16[16,16,640]{2,1,0:T(8,128)(2,1)}), bf16[16,16,640]{2,1,0:T(8,128)(2,1)S(1)}, u32[]{:S(2)}, u32[]{:S(2)}) async-start(bf16[16,16,640]{2,1,0:T(8,128)(2,1)} %add_convert_fusion), calls=%async_computation.4 | async-start | bytes 655360 | tf_op jit(solution)/shard_map/all_to_all | solution.py:429
  94.9 11.0 %multiply_subtract_fusion = (f32[160,7168]{1,0:T(8,128)}, f32[160,7168]{1,0:T(8,128)}, f32[160,7168]{1,0:T(8,128)}) fusion(f32[160,7168]{1,0:T(8,128)} %param.16, bf16[160,7168]{1,0:T(8,128)(2,1)} %param.19, f32[160,7168]{1,0:T(8,128)} %param.17, f32[160,7168]{1,0:T(8,128)} %param.18), kind=kLoop, calls=%fused_computation.42 | loop fusion | flops 18350080 | bytes 29818880 | tf_op jit(solution)/shard_map/sub | solution.py:38
  105.9 0.7 all-to-all-done.4.sums_ref
  106.6 0.7 finish.1
  (13 shorter events, 0.2 us)
Async XLA Ops:
  4.5 15.1 %all-to-all-start.1 = ((bf16[32,16,128]{2,1,0:T(8,128)(2,1)}), bf16[32,16,128]{2,1,0:T(8,128)(2,1)S(1)}, u32[]{:S(2)}, u32[]{:S(2)}) async-start(bf16[32,16,128]{2,1,0:T(8,128)(2,1)} %get-tuple-element.217), calls=%async_computation.1 | async-start | bytes 262144 | tf_op jit(solution)/shard_map/all_to_all | solution.py:458
  11.8 7.5 %copy-start = (s32[64,128]{1,0:T(8,128)S(1)}, s32[64,128]{1,0:T(8,128)}, u32[]{:S(2)}) copy-start(s32[64,128]{1,0:T(8,128)} %get-tuple-element.243.place_ref) | copy-start | bytes 98308
  11.8 10.4 %copy-start.1 = (f32[5120]{0:T(1024)S(1)}, f32[5120]{0:T(1024)}, u32[]{:S(2)}) copy-start(f32[5120]{0:T(1024)} %param.24) | copy-start | bytes 61444
  23.2 2.5 %collective-permute-start = (f32[2,2,2,4,8,896]{5,4,3,2,1,0:T(8,128)S(1)}, f32[2,2,2,4,8,896]{5,4,3,2,1,0:T(8,128)S(1)}, u32[]{:S(2)}, u32[]{:S(2)}) collective-permute-start(f32[2,2,2,4,8,896]{5,4,3,2,1,0:T(8,128)S(1)} %get-tuple-element.224), channel_id=1, source_target_pairs={{0,8},{1,9},{2,10},{3,11},{4,12},{5,13},{6,14},{7,15},{8,0},{9,1},... | collective-permute-start | bytes 2752520 | tf_op jit(solution)/shard_map/ppermute | solution.py:420
  25.8 7.8 %collective-permute-start.1 = (f32[2,4,8,896]{3,2,1,0:T(8,128)S(1)}, f32[2,4,8,896]{3,2,1,0:T(8,128)S(1)}, u32[]{:S(2)}, u32[]{:S(2)}) collective-permute-start(f32[2,4,8,896]{3,2,1,0:T(8,128)S(1)} %get-tuple-element.273), channel_id=1, source_target_pairs={{0,16},{1,17},{2,18},{3,19},{4,20},{5,21},{6,22},{7,23},{8,24},{9,... | collective-permute-start | bytes 688136 | tf_op jit(solution)/shard_map/ppermute | solution.py:426
  27.6 7.4 %collective-permute-start.3 = (f32[2,4,8,896]{3,2,1,0:T(8,128)S(1)}, f32[2,4,8,896]{3,2,1,0:T(8,128)S(1)}, u32[]{:S(2)}, u32[]{:S(2)}) collective-permute-start(f32[2,4,8,896]{3,2,1,0:T(8,128)S(1)} %get-tuple-element.274), channel_id=1, source_target_pairs={{0,1},{1,0},{2,3},{3,2},{4,5},{5,4},{6,7},{7,6},{8,9},{9,8},{10,11... | collective-permute-start | bytes 688136 | tf_op jit(solution)/shard_map/ppermute | solution.py:426
  35.1 4.9 %collective-permute-start.4 = (f32[4,8,896]{2,1,0:T(8,128)S(1)}, f32[4,8,896]{2,1,0:T(8,128)S(1)}, u32[]{:S(2)}, u32[]{:S(2)}) collective-permute-start(f32[4,8,896]{2,1,0:T(8,128)S(1)} %slice_bitcast_fusion), channel_id=1, source_target_pairs={{0,16},{1,17},{2,18},{3,19},{4,20},{5,21},{6,22},{7,23},{8,24},{9,... | collective-permute-start | bytes 344072 | tf_op jit(solution)/shard_map/ppermute | solution.py:426
  35.5 4.9 %collective-permute-start.2 = (f32[4,8,896]{2,1,0:T(8,128)S(1)}, f32[4,8,896]{2,1,0:T(8,128)S(1)}, u32[]{:S(2)}, u32[]{:S(2)}) collective-permute-start(f32[4,8,896]{2,1,0:T(8,128)S(1)} %slice_bitcast_fusion.2), channel_id=1, source_target_pairs={{0,1},{1,0},{2,3},{3,2},{4,5},{5,4},{6,7},{7,6},{8,9},{9,8},{10,11... | collective-permute-start | bytes 344072 | tf_op jit(solution)/shard_map/ppermute | solution.py:426
  40.4 7.0 %collective-permute-start.5 = (f32[2,16,896]{2,1,0:T(8,128)S(1)}, f32[2,16,896]{2,1,0:T(8,128)S(1)}, u32[]{:S(2)}, u32[]{:S(2)}) collective-permute-start(f32[2,16,896]{2,1,0:T(8,128)S(1)} %pad_maximum_fusion), channel_id=1, source_target_pairs={{0,4},{1,5},{2,6},{3,7},{4,0},{5,1},{6,2},{7,3},{8,12},{9,13},{10,... | collective-permute-start | bytes 344072 | tf_op jit(solution)/shard_map/ppermute | solution.py:426
  47.4 4.2 %collective-permute-start.6 = (f32[1,16,896]{2,1,0:T(8,128)S(1)}, f32[1,16,896]{2,1,0:T(8,128)S(1)}, u32[]{:S(2)}, u32[]{:S(2)}) collective-permute-start(f32[1,16,896]{2,1,0:T(8,128)S(1)} %slice.90), channel_id=1, source_target_pairs={{0,2},{1,3},{2,0},{3,1},{4,6},{5,7},{6,4},{7,5},{8,10},{9,11},{10,... | collective-permute-start | bytes 172040 | tf_op jit(solution)/shard_map/ppermute | solution.py:426
  73.4 13.4 %all-to-all-start.3 = ((bf16[32,16,256]{2,1,0:T(8,128)(2,1)}), bf16[32,16,256]{2,1,0:T(8,128)(2,1)S(1)}, u32[]{:S(2)}, u32[]{:S(2)}) async-start(bf16[32,16,256]{2,1,0:T(8,128)(2,1)} %attend.1), calls=%async_computation.3 | async-start | bytes 524288 | tf_op jit(solution)/shard_map/all_to_all | solution.py:543
  87.8 2.2 %collective-permute-start.7 = (f32[16,16,640]{2,1,0:T(8,128)S(1)}, f32[16,16,640]{2,1,0:T(8,128)S(1)}, u32[]{:S(2)}, u32[]{:S(2)}) collective-permute-start(f32[16,16,640]{2,1,0:T(8,128)S(1)} %get-tuple-element.226), channel_id=1, source_target_pairs={{0,8},{1,9},{2,10},{3,11},{4,12},{5,13},{6,14},{7,15},{8,0},{9,1},... | collective-permute-start | bytes 1966088 | tf_op jit(solution)/shard_map/ppermute | solution.py:420
  90.7 15.8 %all-to-all-start.4 = ((bf16[16,16,640]{2,1,0:T(8,128)(2,1)}), bf16[16,16,640]{2,1,0:T(8,128)(2,1)S(1)}, u32[]{:S(2)}, u32[]{:S(2)}) async-start(bf16[16,16,640]{2,1,0:T(8,128)(2,1)} %add_convert_fusion), calls=%async_computation.4 | async-start | bytes 655360 | tf_op jit(solution)/shard_map/all_to_all | solution.py:429

commit v6 on v5

--- a/solution.py
+++ b/solution.py
@@ -217,7 +217,7 @@
             ((GROUP + 1) * HEAD, width + kv_width + g * HEAD, HEAD),
         )
         away = g ^ my_tp
-        in_y, in_z = away % 2, away // 2
+        in_y, in_z = away % 2, away // 4 + away // 2 % 2 * 2
         for to, at, size in spans:
             part = dot(at, size)
             cols = slice(to, to + size)
@@ -507,11 +507,11 @@
     halves = fold(halves, ((2, 0), (0, 1)))
     halves = fold(halves, ((0, 1), (2, 0)))
     total = jnp.concatenate(halves, axis=1)
-    flip = tp // 2
+    flip = 2
     while total.shape[0] > 1:
         count = total.shape[0] // 2
         total = total[:count] + neighbour(total[count:], (0, flip))
-        flip //= 2
+        flip *= 2
     projected = total[0].astype(BF16)
     joined = lax.all_to_all(
         jnp.broadcast_to(projected[None], (tp,) + projected.shape), "tp", 0, 0, tiled=True

time: 108 us -> 107 us (level)
  waiting for transfers between devices: 24.4 us -> 21.8 us
  starting transfers between devices: 23.6 us -> 25.3 us
    ppermute x6, waiting for transfers between devices: 16.9 us -> 14.3 us  [neighbour(): return lax.ppermute(value, BOTH, pairs)]
    ppermute x6, starting transfers between devices: 8.82 us -> 10.4 us  [neighbour(): return lax.ppermute(value, BOTH, pairs)]
where the time goes in v6:
time: 107 us; the launch traced here: 106 us
  other arithmetic  27.4 us (26%)
  starting transfers between devices  25.3 us (24%)
  waiting for transfers between devices  21.8 us (20%)
  Pallas kernels  14.4 us (13%)
  blocking collectives  13.4 us (13%)
  between operations  3.44 us (3%)
    ppermute x6, waiting for transfers between devices, neighbour(): return lax.ppermute(value, BOTH, pairs)  14.3 us
    all_to_all x1, blocking collectives, on_device_partial(): lax.all_to_all(jnp.broadcast_to(projected[None], (tp,) + projected.shape)...  13.4 us
    sub x1, other arithmetic, adamw(): master_new = master - LEARN_RATE * (update + WEIGHT_DECAY * master)  11 us
    ppermute x6, starting transfers between devices, neighbour(): return lax.ppermute(value, BOTH, pairs)  10.4 us
    pallas_call x1, Pallas kernels, on_device_partial(): pl.pallas_call(functools.partial(attend_kernel, dp, tp), out_shape=jax.Sh...  7.98 us
    convert_element_type x1, other arithmetic, on_device_partial(): out_half = out_master_new.astype(BF16)  7.97 us
    convert_element_type x1, other arithmetic, on_device_partial(): adamw(qkv_master, qkv_first, qkv_second, qkv_grad)[0].astype(BF16)  7.5 us
    all_to_all x1, starting transfers between devices, on_device_partial(): arrived = lax.all_to_all(message, BOTH, 0, 0, tiled=True)  7.3 us
  transfers between devices with their start and end apart: 11, of which 10 were waited for; matrix products, arithmetic and copies ran while one was open for 25% of the time, Pallas kernels for 0%

profile of v6, /device:TPU:0, one launch (start us, length us, event | category | flops | bytes accessed | tf_op | source)
XLA Modules:
  0.0 106.0 jit_solution(10654323789833287133)
XLA Ops:
  0.6 3.8 %lookup.1 = (bf16[32,16,128]{2,1,0:T(8,128)(2,1)}, bf16[64,5120]{1,0:T(8,128)(2,1)S(1)}, s32[64,128]{1,0:T(8,128)}, s32[1]{0:T(128)}) custom-call(s32[2,32]{1,0:T(2,128)} %bitcast.44, bf16[2376,5120]{1,0:T(8,128)(2,1)} %table_ref.1, f32[1,5120]{1,0:T(1,128)} %bitcast.43), custom_call_target="tpu_custom_call" | custom-call | tf_op jit(solution)/shard_map/lookup/pallas_call | solution.py:431
  4.5 7.3 %all-to-all-start.1 = ((bf16[32,16,128]{2,1,0:T(8,128)(2,1)}), bf16[32,16,128]{2,1,0:T(8,128)(2,1)S(1)}, u32[]{:S(2)}, u32[]{:S(2)}) async-start(bf16[32,16,128]{2,1,0:T(8,128)(2,1)} %get-tuple-element.217), calls=%async_computation.1 | async-start | bytes 262144 | tf_op jit(solution)/shard_map/all_to_all | solution.py:458
  11.8 0.0 copy-start
  11.8 0.0 copy-start.1
  11.8 7.5 %fusion.19.weight_ref = bf16[160,7168]{1,0:T(8,128)(2,1)S(1)} fusion(f32[160,7168]{1,0:T(8,128)} %param.16, f32[160,7168]{1,0:T(8,128)} %param.18, bf16[160,7168]{1,0:T(8,128)(2,1)} %param.19, f32[160,7168]{1,0:T(8,128)} %param.17), kind=kLoop, calls=%fused_computation.43 | loop fusion | flops 19496960 | bytes 18350080 | tf_op jit(solution)/shard_map/convert_element_type | solution.py:480
  19.3 0.0 copy-done
  19.3 0.1 copy.25
  19.4 0.1 copy.27
  19.5 0.1 copy.26
  19.6 0.0 all-to-all-done.1.msg_ref
  22.2 0.0 copy-done.1
  22.3 1.0 project.1
  23.2 0.3 collective-permute-start
  23.5 2.2 %collective-permute-done = f32[2,2,2,4,8,896]{5,4,3,2,1,0:T(8,128)S(1)} collective-permute-done((f32[2,2,2,4,8,896]{5,4,3,2,1,0:T(8,128)S(1)}, f32[2,2,2,4,8,896]{5,4,3,2,1,0:T(8,128)S(1)}, u32[]{:S(2)}, u32[]{:S(2)}) %collective-permute-start) | collective-permute-done | bytes 917536 | tf_op jit(solution)/shard_map/ppermute | solution.py:420
  25.8 1.8 %collective-permute-start.1 = (f32[2,4,8,896]{3,2,1,0:T(8,128)S(1)}, f32[2,4,8,896]{3,2,1,0:T(8,128)S(1)}, u32[]{:S(2)}, u32[]{:S(2)}) collective-permute-start(f32[2,4,8,896]{3,2,1,0:T(8,128)S(1)} %get-tuple-element.273), channel_id=1, source_target_pairs={{0,16},{1,17},{2,18},{3,19},{4,20},{5,21},{6,22},{7,23},{8,24},{9,... | collective-permute-start | bytes 688136 | tf_op jit(solution)/shard_map/ppermute | solution.py:426
  27.6 1.5 %collective-permute-start.3 = (f32[2,4,8,896]{3,2,1,0:T(8,128)S(1)}, f32[2,4,8,896]{3,2,1,0:T(8,128)S(1)}, u32[]{:S(2)}, u32[]{:S(2)}) collective-permute-start(f32[2,4,8,896]{3,2,1,0:T(8,128)S(1)} %get-tuple-element.274), channel_id=1, source_target_pairs={{0,1},{1,0},{2,3},{3,2},{4,5},{5,4},{6,7},{7,6},{8,9},{9,8},{10,11... | collective-permute-start | bytes 688136 | tf_op jit(solution)/shard_map/ppermute | solution.py:426
  29.1 4.5 %collective-permute-done.1 = f32[2,4,8,896]{3,2,1,0:T(8,128)S(1)} collective-permute-done((f32[2,4,8,896]{3,2,1,0:T(8,128)S(1)}, f32[2,4,8,896]{3,2,1,0:T(8,128)S(1)}, u32[]{:S(2)}, u32[]{:S(2)}) %collective-permute-start.1) | collective-permute-done | bytes 229408 | tf_op jit(solution)/shard_map/ppermute | solution.py:426
  33.6 1.4 %collective-permute-done.3 = f32[2,4,8,896]{3,2,1,0:T(8,128)S(1)} collective-permute-done((f32[2,4,8,896]{3,2,1,0:T(8,128)S(1)}, f32[2,4,8,896]{3,2,1,0:T(8,128)S(1)}, u32[]{:S(2)}, u32[]{:S(2)}) %collective-permute-start.3) | collective-permute-done | bytes 229408 | tf_op jit(solution)/shard_map/ppermute | solution.py:426
  35.0 0.1 fusion.27
  35.1 0.4 collective-permute-start.4
  35.5 1.7 %collective-permute-start.2 = (f32[4,8,896]{2,1,0:T(8,128)S(1)}, f32[4,8,896]{2,1,0:T(8,128)S(1)}, u32[]{:S(2)}, u32[]{:S(2)}) collective-permute-start(f32[4,8,896]{2,1,0:T(8,128)S(1)} %slice_bitcast_fusion.2), channel_id=1, source_target_pairs={{0,1},{1,0},{2,3},{3,2},{4,5},{5,4},{6,7},{7,6},{8,9},{9,8},{10,11... | collective-permute-start | bytes 344072 | tf_op jit(solution)/shard_map/ppermute | solution.py:426
  37.3 2.7 %collective-permute-done.4 = f32[4,8,896]{2,1,0:T(8,128)S(1)} collective-permute-done((f32[4,8,896]{2,1,0:T(8,128)S(1)}, f32[4,8,896]{2,1,0:T(8,128)S(1)}, u32[]{:S(2)}, u32[]{:S(2)}) %collective-permute-start.4) | collective-permute-done | bytes 114720 | tf_op jit(solution)/shard_map/ppermute | solution.py:426
  40.0 0.4 collective-permute-done.2
  40.4 1.7 %collective-permute-start.5 = (f32[2,16,896]{2,1,0:T(8,128)S(1)}, f32[2,16,896]{2,1,0:T(8,128)S(1)}, u32[]{:S(2)}, u32[]{:S(2)}) collective-permute-start(f32[2,16,896]{2,1,0:T(8,128)S(1)} %pad_maximum_fusion), channel_id=1, source_target_pairs={{0,2},{1,3},{2,0},{3,1},{4,6},{5,7},{6,4},{7,5},{8,10},{9,11},{10,... | collective-permute-start | bytes 344072 | tf_op jit(solution)/shard_map/ppermute | solution.py:426
  42.2 3.1 %collective-permute-done.5 = f32[2,16,896]{2,1,0:T(8,128)S(1)} collective-permute-done((f32[2,16,896]{2,1,0:T(8,128)S(1)}, f32[2,16,896]{2,1,0:T(8,128)S(1)}, u32[]{:S(2)}, u32[]{:S(2)}) %collective-permute-start.5) | collective-permute-done | bytes 114720 | tf_op jit(solution)/shard_map/ppermute | solution.py:426
  45.3 3.3 %collective-permute-start.6 = (f32[1,16,896]{2,1,0:T(8,128)S(1)}, f32[1,16,896]{2,1,0:T(8,128)S(1)}, u32[]{:S(2)}, u32[]{:S(2)}) collective-permute-start(f32[1,16,896]{2,1,0:T(8,128)S(1)} %slice.90), channel_id=1, source_target_pairs={{0,4},{1,5},{2,6},{3,7},{4,0},{5,1},{6,2},{7,3},{8,12},{9,13},{10,... | collective-permute-start | bytes 172040 | tf_op jit(solution)/shard_map/ppermute | solution.py:426
  48.6 2.2 %collective-permute-done.6 = f32[1,16,896]{2,1,0:T(8,128)S(1)} collective-permute-done((f32[1,16,896]{2,1,0:T(8,128)S(1)}, f32[1,16,896]{2,1,0:T(8,128)S(1)}, u32[]{:S(2)}, u32[]{:S(2)}) %collective-permute-start.6) | collective-permute-done | bytes 57376 | tf_op jit(solution)/shard_map/ppermute | solution.py:426
  50.8 13.4 %all_to_all.32.qkv_ref = bf16[8,16,896]{2,1,0:T(8,128)(2,1)} all-to-all(bf16[8,16,896]{2,1,0:T(8,128)(2,1)S(1)} %broadcast_in_dim.21), channel_id=1, replica_groups=mesh['dp'=4,'tp'=8] {'tp'}, dimensions={0} | all-to-all | bytes 458752 | tf_op jit(solution)/shard_map/all_to_all | solution.py:516
  64.1 8.0 %attend.1 = bf16[32,16,256]{2,1,0:T(8,128)(2,1)} custom-call(s32[8]{0:T(128)} %lengths_ref.1, bf16[8,16,896]{2,1,0:T(8,128)(2,1)} %all_to_all.32.qkv_ref, bf16[8,256,1024]{2,1,0:T(8,128)(2,1)} %keys_ref.1, bf16[8,256,1024]{2,1,0:T(8,128)(2,1)} %values_ref.1), custom_call_target="tpu_custom_call" | custom-call | tf_op jit(solution)/shard_map/attend/pallas_call | solution.py:520
  72.1 3.0 %all-to-all-start.3 = ((bf16[32,16,256]{2,1,0:T(8,128)(2,1)}), bf16[32,16,256]{2,1,0:T(8,128)(2,1)S(1)}, u32[]{:S(2)}, u32[]{:S(2)}) async-start(bf16[32,16,256]{2,1,0:T(8,128)(2,1)} %attend.1), calls=%async_computation.3 | async-start | bytes 524288 | tf_op jit(solution)/shard_map/all_to_all | solution.py:543
  75.1 8.0 %fusion.36 = (bf16[160,5120]{1,0:T(8,128)(2,1)S(1)}, f32[160,5120]{1,0:T(8,128)}, f32[160,5120]{1,0:T(8,128)}, f32[160,5120]{1,0:T(8,128)}) fusion(f32[160,5120]{1,0:T(8,128)} %param.20, bf16[160,5120]{1,0:T(8,128)(2,1)} %param.23, f32[160,5120]{1,0:T(8,128)} %param.21, f32[160,5120]{1,0:T(8,128)} %param.22), kind=kLoop, calls=%fused_computation.75 | loop fusion | flops 13926400 | bytes 22937600 | tf_op jit(solution)/shard_map/convert_element_type | solution.py:484
  83.1 2.5 %all-to-all-done.3.msg_ref = bf16[32,16,256]{2,1,0:T(8,128)(2,1)S(1)} async-done(((bf16[32,16,256]{2,1,0:T(8,128)(2,1)}), bf16[32,16,256]{2,1,0:T(8,128)(2,1)S(1)}, u32[]{:S(2)}, u32[]{:S(2)}) %all-to-all-start.3) | async-done | bytes 262176 | tf_op jit(solution)/shard_map/all_to_all | solution.py:543
  85.6 1.0 output.1
  86.6 0.1 collective-permute-start.7
  86.6 2.1 %collective-permute-done.7 = f32[16,16,640]{2,1,0:T(8,128)S(1)} collective-permute-done((f32[16,16,640]{2,1,0:T(8,128)S(1)}, f32[16,16,640]{2,1,0:T(8,128)S(1)}, u32[]{:S(2)}, u32[]{:S(2)}) %collective-permute-start.7) | collective-permute-done | bytes 655392 | tf_op jit(solution)/shard_map/ppermute | solution.py:420
  88.7 0.8 add_convert_fusion
  89.5 4.2 %all-to-all-start.4 = ((bf16[16,16,640]{2,1,0:T(8,128)(2,1)}), bf16[16,16,640]{2,1,0:T(8,128)(2,1)S(1)}, u32[]{:S(2)}, u32[]{:S(2)}) async-start(bf16[16,16,640]{2,1,0:T(8,128)(2,1)} %add_convert_fusion), calls=%async_computation.4 | async-start | bytes 655360 | tf_op jit(solution)/shard_map/all_to_all | solution.py:429
  93.7 11.0 %multiply_subtract_fusion = (f32[160,7168]{1,0:T(8,128)}, f32[160,7168]{1,0:T(8,128)}, f32[160,7168]{1,0:T(8,128)}) fusion(f32[160,7168]{1,0:T(8,128)} %param.16, bf16[160,7168]{1,0:T(8,128)(2,1)} %param.19, f32[160,7168]{1,0:T(8,128)} %param.17, f32[160,7168]{1,0:T(8,128)} %param.18), kind=kLoop, calls=%fused_computation.42 | loop fusion | flops 18350080 | bytes 29818880 | tf_op jit(solution)/shard_map/sub | solution.py:38
  104.7 0.7 all-to-all-done.4.sums_ref
  105.3 0.7 finish.1
  (13 shorter events, 0.2 us)
Async XLA Ops:
  4.5 15.1 %all-to-all-start.1 = ((bf16[32,16,128]{2,1,0:T(8,128)(2,1)}), bf16[32,16,128]{2,1,0:T(8,128)(2,1)S(1)}, u32[]{:S(2)}, u32[]{:S(2)}) async-start(bf16[32,16,128]{2,1,0:T(8,128)(2,1)} %get-tuple-element.217), calls=%async_computation.1 | async-start | bytes 262144 | tf_op jit(solution)/shard_map/all_to_all | solution.py:458
  11.8 7.5 %copy-start = (s32[64,128]{1,0:T(8,128)S(1)}, s32[64,128]{1,0:T(8,128)}, u32[]{:S(2)}) copy-start(s32[64,128]{1,0:T(8,128)} %get-tuple-element.243.place_ref) | copy-start | bytes 98308
  11.8 10.4 %copy-start.1 = (f32[5120]{0:T(1024)S(1)}, f32[5120]{0:T(1024)}, u32[]{:S(2)}) copy-start(f32[5120]{0:T(1024)} %param.24) | copy-start | bytes 61444
  23.2 2.5 %collective-permute-start = (f32[2,2,2,4,8,896]{5,4,3,2,1,0:T(8,128)S(1)}, f32[2,2,2,4,8,896]{5,4,3,2,1,0:T(8,128)S(1)}, u32[]{:S(2)}, u32[]{:S(2)}) collective-permute-start(f32[2,2,2,4,8,896]{5,4,3,2,1,0:T(8,128)S(1)} %get-tuple-element.224), channel_id=1, source_target_pairs={{0,8},{1,9},{2,10},{3,11},{4,12},{5,13},{6,14},{7,15},{8,0},{9,1},... | collective-permute-start | bytes 2752520 | tf_op jit(solution)/shard_map/ppermute | solution.py:420
  25.8 7.8 %collective-permute-start.1 = (f32[2,4,8,896]{3,2,1,0:T(8,128)S(1)}, f32[2,4,8,896]{3,2,1,0:T(8,128)S(1)}, u32[]{:S(2)}, u32[]{:S(2)}) collective-permute-start(f32[2,4,8,896]{3,2,1,0:T(8,128)S(1)} %get-tuple-element.273), channel_id=1, source_target_pairs={{0,16},{1,17},{2,18},{3,19},{4,20},{5,21},{6,22},{7,23},{8,24},{9,... | collective-permute-start | bytes 688136 | tf_op jit(solution)/shard_map/ppermute | solution.py:426
  27.6 7.4 %collective-permute-start.3 = (f32[2,4,8,896]{3,2,1,0:T(8,128)S(1)}, f32[2,4,8,896]{3,2,1,0:T(8,128)S(1)}, u32[]{:S(2)}, u32[]{:S(2)}) collective-permute-start(f32[2,4,8,896]{3,2,1,0:T(8,128)S(1)} %get-tuple-element.274), channel_id=1, source_target_pairs={{0,1},{1,0},{2,3},{3,2},{4,5},{5,4},{6,7},{7,6},{8,9},{9,8},{10,11... | collective-permute-start | bytes 688136 | tf_op jit(solution)/shard_map/ppermute | solution.py:426
  35.1 4.9 %collective-permute-start.4 = (f32[4,8,896]{2,1,0:T(8,128)S(1)}, f32[4,8,896]{2,1,0:T(8,128)S(1)}, u32[]{:S(2)}, u32[]{:S(2)}) collective-permute-start(f32[4,8,896]{2,1,0:T(8,128)S(1)} %slice_bitcast_fusion), channel_id=1, source_target_pairs={{0,16},{1,17},{2,18},{3,19},{4,20},{5,21},{6,22},{7,23},{8,24},{9,... | collective-permute-start | bytes 344072 | tf_op jit(solution)/shard_map/ppermute | solution.py:426
  35.5 4.9 %collective-permute-start.2 = (f32[4,8,896]{2,1,0:T(8,128)S(1)}, f32[4,8,896]{2,1,0:T(8,128)S(1)}, u32[]{:S(2)}, u32[]{:S(2)}) collective-permute-start(f32[4,8,896]{2,1,0:T(8,128)S(1)} %slice_bitcast_fusion.2), channel_id=1, source_target_pairs={{0,1},{1,0},{2,3},{3,2},{4,5},{5,4},{6,7},{7,6},{8,9},{9,8},{10,11... | collective-permute-start | bytes 344072 | tf_op jit(solution)/shard_map/ppermute | solution.py:426
  40.4 4.9 %collective-permute-start.5 = (f32[2,16,896]{2,1,0:T(8,128)S(1)}, f32[2,16,896]{2,1,0:T(8,128)S(1)}, u32[]{:S(2)}, u32[]{:S(2)}) collective-permute-start(f32[2,16,896]{2,1,0:T(8,128)S(1)} %pad_maximum_fusion), channel_id=1, source_target_pairs={{0,2},{1,3},{2,0},{3,1},{4,6},{5,7},{6,4},{7,5},{8,10},{9,11},{10,... | collective-permute-start | bytes 344072 | tf_op jit(solution)/shard_map/ppermute | solution.py:426
  45.3 5.4 %collective-permute-start.6 = (f32[1,16,896]{2,1,0:T(8,128)S(1)}, f32[1,16,896]{2,1,0:T(8,128)S(1)}, u32[]{:S(2)}, u32[]{:S(2)}) collective-permute-start(f32[1,16,896]{2,1,0:T(8,128)S(1)} %slice.90), channel_id=1, source_target_pairs={{0,4},{1,5},{2,6},{3,7},{4,0},{5,1},{6,2},{7,3},{8,12},{9,13},{10,... | collective-permute-start | bytes 172040 | tf_op jit(solution)/shard_map/ppermute | solution.py:426
  72.1 13.4 %all-to-all-start.3 = ((bf16[32,16,256]{2,1,0:T(8,128)(2,1)}), bf16[32,16,256]{2,1,0:T(8,128)(2,1)S(1)}, u32[]{:S(2)}, u32[]{:S(2)}) async-start(bf16[32,16,256]{2,1,0:T(8,128)(2,1)} %attend.1), calls=%async_computation.3 | async-start | bytes 524288 | tf_op jit(solution)/shard_map/all_to_all | solution.py:543
  86.6 2.2 %collective-permute-start.7 = (f32[16,16,640]{2,1,0:T(8,128)S(1)}, f32[16,16,640]{2,1,0:T(8,128)S(1)}, u32[]{:S(2)}, u32[]{:S(2)}) collective-permute-start(f32[16,16,640]{2,1,0:T(8,128)S(1)} %get-tuple-element.226), channel_id=1, source_target_pairs={{0,8},{1,9},{2,10},{3,11},{4,12},{5,13},{6,14},{7,15},{8,0},{9,1},... | collective-permute-start | bytes 1966088 | tf_op jit(solution)/shard_map/ppermute | solution.py:420
  89.5 15.8 %all-to-all-start.4 = ((bf16[16,16,640]{2,1,0:T(8,128)(2,1)}), bf16[16,16,640]{2,1,0:T(8,128)(2,1)S(1)}, u32[]{:S(2)}, u32[]{:S(2)}) async-start(bf16[16,16,640]{2,1,0:T(8,128)(2,1)} %add_convert_fusion), calls=%async_computation.4 | async-start | bytes 655360 | tf_op jit(solution)/shard_map/all_to_all | solution.py:429
